TPU v7x, 512 devices: a whole 4x8x8 slice. The times are simulated.
512 devices in a mesh: expert: 32 (over y_hi, z), dp: 16 (over x, y_lo, core).
Axes of the slice: x: 4, y: 8 (y_hi: 4, y_lo: 2; y = y_hi * 2 + y_lo), z: 8, core: 2. Of those that a mesh axis runs over, the one named last changes fastest.
Arguments:
- tokens: bfloat16 [65536, 2560], P(('expert', 'dp')), may hold values from -6 to 6
- cotangent: bfloat16 [65536, 2560], P(('expert', 'dp')), may hold values from -6 to 6
- gates: bfloat16 [65536, 2], P(('expert', 'dp')), may hold values from 0.099609375 to 1
- routes: int32 [65536, 2], P(('expert', 'dp')), may hold values from -1 to 7, as said below
- gate_proj: bfloat16 [32, 192, 2560], P('expert', 'dp'), may hold values from -0.125 to 0.125
- up_proj: bfloat16 [32, 192, 2560], P('expert', 'dp'), may hold values from -0.125 to 0.125
- down_proj: bfloat16 [32, 192, 2560], P('expert', 'dp'), may hold values from -0.21875 to 0.21875
Outputs:
- grad_tokens: bfloat16 [65536, 2560], P(('expert', 'dp'))
- grad_gates: float32 [65536, 2], P(('expert', 'dp'))
- grad_gate_proj: bfloat16 [32, 192, 2560], P('expert', 'dp')
- grad_up_proj: bfloat16 [32, 192, 2560], P('expert', 'dp')
- grad_down_proj: bfloat16 [32, 192, 2560], P('expert', 'dp')
Inputs may be any that keep to these rules, and one draw needn't show every extreme that they name: `routes`: each row lists 1 to 2 different experts in its first entries and -1 in the others.
All inputs are finite; a program needn't handle non-finite values.
Results may differ from a plain program's by a relative error of at most 0.0085.
Values may be sent and summed in bfloat16 or wider, within the bound.
A program may use at most 64 MiB of HBM per device.

v0:
```python
import jax
import jax.numpy as jnp
from jax import lax
from jax.sharding import PartitionSpec as P

GROUP = 4


def slot_tables(route_block, experts, capacity):
    expert_range = jnp.arange(experts, dtype=jnp.int32)
    named = route_block[:, :, None] == expert_range[None, None, :]
    hits = jnp.sum(named.astype(jnp.int32), axis=1)
    before = jnp.cumsum(hits, axis=0) - hits
    rank_pick = jnp.sum(jnp.where(named, before[:, None, :], 0), axis=2)
    kept_slot = (route_block >= 0) & (rank_pick < capacity)
    slot_ids = jnp.where(kept_slot, route_block * capacity + rank_pick, -1)
    return slot_ids


def unit_pass(rows_x, scaled_dy, gate_rows, up_rows, down_rows):
    contract = (((1,), (1,)), ((), ()))
    pre_gate = lax.dot_general(rows_x, gate_rows, contract, preferred_element_type=jnp.float32)
    pre_up = lax.dot_general(rows_x, up_rows, contract, preferred_element_type=jnp.float32)
    sigmoid_gate = jax.nn.sigmoid(pre_gate)
    activated = pre_gate * sigmoid_gate
    hidden = (activated * pre_up).astype(jnp.bfloat16)
    outward = jnp.dot(hidden, down_rows, preferred_element_type=jnp.float32)
    grad_hidden = lax.dot_general(
        scaled_dy, down_rows, contract, preferred_element_type=jnp.float32
    )
    grad_pre_gate = (
        grad_hidden * pre_up * sigmoid_gate * (1.0 + pre_gate * (1.0 - sigmoid_gate))
    ).astype(jnp.bfloat16)
    grad_pre_up = (grad_hidden * activated).astype(jnp.bfloat16)
    slot_grad = jnp.dot(grad_pre_gate, gate_rows, preferred_element_type=jnp.float32) + jnp.dot(
        grad_pre_up, up_rows, preferred_element_type=jnp.float32
    )
    return (hidden, grad_pre_gate, grad_pre_up, outward, slot_grad)


def spread_out(buffer, experts, capacity):
    shaped = buffer.reshape((experts, 1, capacity) + buffer.shape[1:])
    copies = jnp.broadcast_to(shaped, (experts, GROUP, capacity) + buffer.shape[1:])
    return copies.reshape((experts * GROUP, capacity) + buffer.shape[1:])


def per_device(tokens, cotangent, gates, routes, gate_proj, up_proj, down_proj):
    tok_rows, model_width = tokens.shape
    members = lax.axis_size("expert")
    experts = members // GROUP
    capacity = max(2, tok_rows // experts)
    slot_count = experts * capacity
    slot_ids = slot_tables(routes, experts, capacity)
    slot_range = jnp.arange(slot_count, dtype=jnp.int32)
    picked = slot_ids[None, :, :] == slot_range[:, None, None]
    placing = jnp.any(picked, axis=2)
    place_bf = placing.astype(jnp.bfloat16)
    sent_x = jnp.dot(place_bf, tokens, preferred_element_type=jnp.float32).astype(jnp.bfloat16)
    sent_dy = jnp.dot(place_bf, cotangent, preferred_element_type=jnp.float32).astype(jnp.bfloat16)
    sent_gate = jnp.sum(
        jnp.where(picked, gates.astype(jnp.float32)[None, :, :], 0.0), axis=(1, 2)
    ).astype(jnp.bfloat16)
    got_x, got_dy, got_gate = (
        lax.all_to_all(
            spread_out(sent_x, experts, capacity), "expert", split_axis=0, concat_axis=0, tiled=True
        ),
        lax.all_to_all(
            spread_out(sent_dy, experts, capacity),
            "expert",
            split_axis=0,
            concat_axis=0,
            tiled=True,
        ),
        lax.all_to_all(
            spread_out(sent_gate, experts, capacity),
            "expert",
            split_axis=0,
            concat_axis=0,
            tiled=True,
        ),
    )
    rows_x = got_x.reshape(-1, model_width)
    rows_dy = got_dy.reshape(-1, model_width)
    rows_gate = got_gate.reshape(-1).astype(jnp.float32)
    scaled_dy = (rows_gate[:, None] * rows_dy.astype(jnp.float32)).astype(jnp.bfloat16)
    full_gate, full_up, full_down = (
        lax.all_gather(gate_proj, "dp", axis=1, tiled=True),
        lax.all_gather(up_proj, "dp", axis=1, tiled=True),
        lax.all_gather(down_proj, "dp", axis=1, tiled=True),
    )
    hidden, grad_pre_gate, grad_pre_up, outward, slot_grad = unit_pass(
        rows_x, scaled_dy, full_gate[0], full_up[0], full_down[0]
    )
    gate_part = jnp.sum(rows_dy.astype(jnp.float32) * outward, axis=1).astype(jnp.bfloat16)
    slot_part = slot_grad.astype(jnp.bfloat16)
    contract_rows = (((0,), (0,)), ((), ()))
    term_gate = lax.dot_general(
        grad_pre_gate, rows_x, contract_rows, preferred_element_type=jnp.float32
    )
    term_up = lax.dot_general(
        grad_pre_up, rows_x, contract_rows, preferred_element_type=jnp.float32
    )
    term_down = lax.dot_general(
        hidden, scaled_dy, contract_rows, preferred_element_type=jnp.float32
    )
    whole_term = jnp.stack([term_gate, term_up, term_down], axis=1).astype(jnp.bfloat16)
    parted = whole_term.reshape(lax.axis_size("dp"), gate_proj.shape[1], 3, model_width)
    swapped = lax.all_to_all(parted, "dp", split_axis=0, concat_axis=0, tiled=True)
    shares = jnp.sum(swapped.astype(jnp.float32), axis=0)
    weight_grads = shares.astype(jnp.bfloat16)
    back_grad, back_gate = (
        lax.all_to_all(
            slot_part.reshape(members, capacity, model_width),
            "expert",
            split_axis=0,
            concat_axis=0,
            tiled=True,
        ),
        lax.all_to_all(
            gate_part.reshape(members, capacity), "expert", split_axis=0, concat_axis=0, tiled=True
        ),
    )
    tiled = jnp.broadcast_to(
        place_bf.reshape(experts, 1, capacity, tok_rows), (experts, GROUP, capacity, tok_rows)
    )
    tiled = tiled.reshape(members * capacity, tok_rows)
    grad_tokens = lax.dot_general(
        tiled,
        back_grad.reshape(members * capacity, model_width),
        contract_rows,
        preferred_element_type=jnp.float32,
    ).astype(jnp.bfloat16)
    gate_sum = jnp.sum(
        back_gate.reshape(experts, GROUP, capacity).astype(jnp.float32), axis=1
    ).reshape(slot_count)
    grad_gates = jnp.where(slot_ids >= 0, jnp.take(gate_sum, jnp.maximum(slot_ids, 0), axis=0), 0.0)
    return (
        grad_tokens,
        grad_gates,
        weight_grads[None, :, 0, :],
        weight_grads[None, :, 1, :],
        weight_grads[None, :, 2, :],
    )


def solution(mesh):
    in_specs = (
        P(("expert", "dp"), None),
        P(("expert", "dp"), None),
        P(("expert", "dp"), None),
        P(("expert", "dp"), None),
        P("expert", "dp", None),
        P("expert", "dp", None),
        P("expert", "dp", None),
    )
    out_specs = (
        P(("expert", "dp"), None),
        P(("expert", "dp"), None),
        P("expert", "dp", None),
        P("expert", "dp", None),
        P("expert", "dp", None),
    )
    return jax.shard_map(
        per_device, mesh=mesh, in_specs=in_specs, out_specs=out_specs, check_vma=False
    )
```

profile of v0, /device:TPU:1, one launch (start us, length us, event | category | flops | bytes accessed | tf_op | source)
XLA Modules:
  0.0 463.5 jit_solution(2741525155790413076)
XLA Ops:
  3.1 1.2 broadcast_maximum_fusion
  5.2 16.5 %all-to-all-start = ((bf16[32,1,16]{2,1,0:T(2,128)(2,1)}), bf16[32,1,16]{2,1,0:T(2,128)(2,1)S(1)}, u32[]{:S(2)}, u32[]{:S(2)}) async-start(bf16[32,1,16]{2,1,0:T(2,128)(2,1)} %copy.62), calls=%async_computation | async-start | bytes 32768 | tf_op jit(solution)/shard_map/all_to_all | solution.py:74
  22.1 10.6 %all-to-all-done = bf16[32,1,16]{2,1,0:T(2,128)(2,1)S(1)} async-done(((bf16[32,1,16]{2,1,0:T(2,128)(2,1)}), bf16[32,1,16]{2,1,0:T(2,128)(2,1)S(1)}, u32[]{:S(2)}, u32[]{:S(2)}) %all-to-all-start) | async-done | bytes 1056 | tf_op jit(solution)/shard_map/all_to_all | solution.py:74
  32.7 1.8 broadcast_in_dim.81
  34.5 4.1 all-to-all-start.2
  38.6 2.3 convolution_convert_fusion.5
  40.8 65.5 %all-to-all-done.2 = bf16[32,16,2560]{2,1,0:T(8,128)(2,1)S(1)} async-done(((bf16[32,16,2560]{2,1,0:T(8,128)(2,1)}), bf16[32,16,2560]{2,1,0:T(8,128)(2,1)S(1)}, u32[]{:S(2)}, u32[]{:S(2)}) %all-to-all-start.2) | async-done | bytes 2621472 | tf_op jit(solution)/shard_map/all_to_all | solution.py:64
  106.3 2.9 broadcast_in_dim.79
  109.2 9.9 %all-to-all-start.1 = ((bf16[32,16,2560]{2,1,0:T(8,128)(2,1)}), bf16[32,16,2560]{2,1,0:T(8,128)(2,1)}, u32[]{:S(2)}, u32[]{:S(2)}) async-start(bf16[32,16,2560]{2,1,0:T(8,128)(2,1)} %bitcast.107), calls=%async_computation.1 | async-start | bytes 5242880 | tf_op jit(solution)/shard_map/all_to_all | solution.py:67
  119.5 95.8 %all_gather.9 = bf16[1,192,2560]{2,0,1:T(2,128)(2,1)} all-gather(bf16[1,12,2560]{2,0,1:T(2,128)(2,1)S(1)} %copy.63), channel_id=1, replica_groups=mesh['expert'=32,'dp'=16] {'dp'}, dimensions={1}, use_global_device_ids=true | all-gather | bytes 1044480 | tf_op jit(solution)/shard_map/all_gather | solution.py:89
  215.3 27.8 %all_gather.10 = bf16[1,192,2560]{2,0,1:T(2,128)(2,1)S(1)} all-gather(bf16[1,12,2560]{2,0,1:T(2,128)(2,1)S(1)} %copy.64), channel_id=1, replica_groups=mesh['expert'=32,'dp'=16] {'dp'}, dimensions={1}, use_global_device_ids=true | all-gather | bytes 1044480 | tf_op jit(solution)/shard_map/all_gather | solution.py:88
  243.1 32.3 %all_gather.11 = bf16[1,192,2560]{2,0,1:T(2,128)(2,1)} all-gather(bf16[1,12,2560]{2,0,1:T(2,128)(2,1)S(1)} %copy.65), channel_id=1, replica_groups=mesh['expert'=32,'dp'=16] {'dp'}, dimensions={1}, use_global_device_ids=true | all-gather | bytes 1044480 | tf_op jit(solution)/shard_map/all_gather | solution.py:87
  275.4 1.8 fusion.9
  277.2 2.4 multiply_convert_fusion
  279.6 1.0 fusion.12
  282.1 1.9 fusion.19
  284.1 3.3 fusion.4
  287.4 2.7 fusion
  290.9 18.9 %all-to-all-start.4 = ((bf16[32,1,16]{2,1,0:T(2,128)(2,1)}), bf16[32,1,16]{2,1,0:T(2,128)(2,1)S(1)}, u32[]{:S(2)}, u32[]{:S(2)}) async-start(bf16[32,1,16]{2,1,0:T(2,128)(2,1)} %convert_element_type.144), calls=%async_computation.4 | async-start | bytes 32768 | tf_op jit(solution)/shard_map/all_to_all | solution.py:119
  309.8 5.8 %add_convert_fusion = bf16[512,2560]{1,0:T(8,128)(2,1)} fusion(f32[512,2560]{1,0:T(8,128)} %fusion.4, bf16[1,192,2560]{2,0,1:T(2,128)(2,1)} %copy-done.4, f32[512,192]{0,1:T(8,128)} %copy-done.6, f32[512,192]{0,1:T(8,128)} %copy-done.7), kind=kOutput, calls=%fused_computation.3 | convolution fusion | flops 506527744 | bytes 9633792 | tf_op jit(solution)/shard_map/dot_general | solution.py:35
  315.5 5.2 %all-to-all-done.4 = bf16[32,1,16]{2,1,0:T(2,128)(2,1)S(1)} async-done(((bf16[32,1,16]{2,1,0:T(2,128)(2,1)}), bf16[32,1,16]{2,1,0:T(2,128)(2,1)S(1)}, u32[]{:S(2)}, u32[]{:S(2)}) %all-to-all-start.4) | async-done | bytes 1056 | tf_op jit(solution)/shard_map/all_to_all | solution.py:119
  321.3 6.7 %all-to-all-start.3 = ((bf16[32,16,2560]{2,1,0:T(8,128)(2,1)}), bf16[32,16,2560]{2,1,0:T(8,128)(2,1)}, u32[]{:S(2)}, u32[]{:S(2)}) async-start(bf16[32,16,2560]{2,1,0:T(8,128)(2,1)} %bitcast.104), calls=%async_computation.3 | async-start | bytes 5242880 | tf_op jit(solution)/shard_map/all_to_all | solution.py:112
  329.8 1.7 dot_general.69
  331.5 1.7 fusion.2
  333.9 1.0 copy-done.2
  336.0 3.6 copy.72
  339.6 68.5 %all-to-all-done.3 = bf16[32,16,2560]{2,1,0:T(8,128)(2,1)} async-done(((bf16[32,16,2560]{2,1,0:T(8,128)(2,1)}), bf16[32,16,2560]{2,1,0:T(8,128)(2,1)}, u32[]{:S(2)}, u32[]{:S(2)}) %all-to-all-start.3) | async-done | bytes 2621472 | tf_op jit(solution)/shard_map/all_to_all | solution.py:112
  408.1 4.8 %all-to-all-start.5 = ((bf16[16,12,3,2560]{3,1,2,0:T(8,128)(2,1)}), bf16[16,12,3,2560]{3,1,2,0:T(8,128)(2,1)}, u32[]{:S(2)}, u32[]{:S(2)}) async-start(bf16[16,12,3,2560]{3,1,2,0:T(8,128)(2,1)} %copy.72), calls=%async_computation.5 | async-start | bytes 7864320 | tf_op jit(solution)/shard_map/all_to_all | solution.py:108
  413.4 1.9 gather_fusion
  416.1 3.1 convolution_convert_fusion.3
  419.2 40.7 %all-to-all-done.5 = bf16[16,12,3,2560]{3,1,2,0:T(8,128)(2,1)} async-done(((bf16[16,12,3,2560]{3,1,2,0:T(8,128)(2,1)}), bf16[16,12,3,2560]{3,1,2,0:T(8,128)(2,1)}, u32[]{:S(2)}, u32[]{:S(2)}) %all-to-all-start.5) | async-done | bytes 2949152 | tf_op jit(solution)/shard_map/all_to_all | solution.py:108
  459.9 2.9 reduce_sum.62
  (71 shorter events, 12.2 us)
Async XLA Ops:
  0.6 21.1 %copy-start = (bf16[128,2560]{1,0:T(8,128)(2,1)S(1)}, bf16[128,2560]{1,0:T(8,128)(2,1)}, u32[]{:S(2)}) copy-start(bf16[128,2560]{1,0:T(8,128)(2,1)} %param.7) | copy-start | bytes 1966084
  4.4 17.4 %copy-start.15 = (s32[128,2]{0,1:T(2,128)}, s32[128,2]{0,1:T(2,128)S(1)}, u32[]{:S(2)}) copy-start(s32[128,2]{0,1:T(2,128)S(1)} %get-tuple-element.21) | copy-start | bytes 3076
  5.2 27.5 %all-to-all-start = ((bf16[32,1,16]{2,1,0:T(2,128)(2,1)}), bf16[32,1,16]{2,1,0:T(2,128)(2,1)S(1)}, u32[]{:S(2)}, u32[]{:S(2)}) async-start(bf16[32,1,16]{2,1,0:T(2,128)(2,1)} %copy.62), calls=%async_computation | async-start | bytes 32768 | tf_op jit(solution)/shard_map/all_to_all | solution.py:74
  34.5 71.8 %all-to-all-start.2 = ((bf16[32,16,2560]{2,1,0:T(8,128)(2,1)}), bf16[32,16,2560]{2,1,0:T(8,128)(2,1)S(1)}, u32[]{:S(2)}, u32[]{:S(2)}) async-start(bf16[32,16,2560]{2,1,0:T(8,128)(2,1)} %bitcast.108), calls=%async_computation.2 | async-start | bytes 5242880 | tf_op jit(solution)/shard_map/all_to_all | solution.py:64
  109.2 9.9 %copy-start.10 = (bf16[1,12,2560]{2,1,0:T(8,128)(2,1)S(1)}, bf16[1,12,2560]{2,1,0:T(8,128)(2,1)}, u32[]{:S(2)}) copy-start(bf16[1,12,2560]{2,1,0:T(8,128)(2,1)} %param.11) | copy-start | bytes 184324
  109.2 10.0 %copy-start.11 = (bf16[1,12,2560]{2,1,0:T(8,128)(2,1)S(1)}, bf16[1,12,2560]{2,1,0:T(8,128)(2,1)}, u32[]{:S(2)}) copy-start(bf16[1,12,2560]{2,1,0:T(8,128)(2,1)} %param.12) | copy-start | bytes 184324
  109.2 10.2 %copy-start.12 = (bf16[1,12,2560]{2,1,0:T(8,128)(2,1)S(1)}, bf16[1,12,2560]{2,1,0:T(8,128)(2,1)}, u32[]{:S(2)}) copy-start(bf16[1,12,2560]{2,1,0:T(8,128)(2,1)} %param.13) | copy-start | bytes 184324
  109.2 168.0 %all-to-all-start.1 = ((bf16[32,16,2560]{2,1,0:T(8,128)(2,1)}), bf16[32,16,2560]{2,1,0:T(8,128)(2,1)}, u32[]{:S(2)}, u32[]{:S(2)}) async-start(bf16[32,16,2560]{2,1,0:T(8,128)(2,1)} %bitcast.107), calls=%async_computation.1 | async-start | bytes 5242880 | tf_op jit(solution)/shard_map/all_to_all | solution.py:67
  243.1 32.4 %copy-start.4 = (bf16[1,192,2560]{2,0,1:T(2,128)(2,1)}, bf16[1,192,2560]{2,0,1:T(2,128)(2,1)S(1)}, u32[]{:S(2)}) copy-start(bf16[1,192,2560]{2,0,1:T(2,128)(2,1)S(1)} %all_gather.10) | copy-start | bytes 2949124
  277.2 2.4 copy-start.5
  279.6 1.5 copy-start.1
  279.6 2.5 copy-start.3
  279.6 2.5 copy-start.9
  282.1 1.9 copy-start.6
  284.1 3.3 copy-start.7
  290.9 29.9 %all-to-all-start.4 = ((bf16[32,1,16]{2,1,0:T(2,128)(2,1)}), bf16[32,1,16]{2,1,0:T(2,128)(2,1)S(1)}, u32[]{:S(2)}, u32[]{:S(2)}) async-start(bf16[32,1,16]{2,1,0:T(2,128)(2,1)} %convert_element_type.144), calls=%async_computation.4 | async-start | bytes 32768 | tf_op jit(solution)/shard_map/all_to_all | solution.py:119
  320.7 0.6 copy-start.13
  321.3 86.8 %all-to-all-start.3 = ((bf16[32,16,2560]{2,1,0:T(8,128)(2,1)}), bf16[32,16,2560]{2,1,0:T(8,128)(2,1)}, u32[]{:S(2)}, u32[]{:S(2)}) async-start(bf16[32,16,2560]{2,1,0:T(8,128)(2,1)} %bitcast.104), calls=%async_computation.3 | async-start | bytes 5242880 | tf_op jit(solution)/shard_map/all_to_all | solution.py:112
  331.5 1.7 copy-start.8
  333.2 1.7 copy-start.2
  339.6 73.3 %copy-start.17 = (s32[128,2]{0,1:T(2,128)S(1)}, s32[128,2]{0,1:T(2,128)}, u32[]{:S(2)}) copy-start(s32[128,2]{0,1:T(2,128)} %get-tuple-element.20) | copy-start | bytes 3076
  339.6 73.6 %copy-start.14 = (bf16[32,1,16]{2,1,0:T(2,128)(2,1)S(1)}, bf16[32,1,16]{2,1,0:T(2,128)(2,1)}, u32[]{:S(2)}) copy-start(bf16[32,1,16]{2,1,0:T(2,128)(2,1)} %copy-done.13) | copy-start | bytes 3076
  408.1 51.8 %all-to-all-start.5 = ((bf16[16,12,3,2560]{3,1,2,0:T(8,128)(2,1)}), bf16[16,12,3,2560]{3,1,2,0:T(8,128)(2,1)}, u32[]{:S(2)}, u32[]{:S(2)}) async-start(bf16[16,12,3,2560]{3,1,2,0:T(8,128)(2,1)} %copy.72), calls=%async_computation.5 | async-start | bytes 7864320 | tf_op jit(solution)/shard_map/all_to_all | solution.py:108
  413.4 2.1 copy-start.16
where the time goes:
time: 469 us; the launch traced here: 463 us
  waiting for transfers between devices  190 us (41%)
  blocking collectives  156 us (33%)
  starting transfers between devices  61 us (13%)
  matrix products  25.3 us (5%)
  local copies, waits for them, and re-layouts  19.9 us (4%)
  other arithmetic  9.89 us (2%)
    all_gather x1, blocking collectives, per_device(): lax.all_gather(down_proj, 'dp', axis=1, tiled=True)  95.8 us
    all_to_all x1, waiting for transfers between devices, per_device(): lax.all_to_all(slot_part.reshape(members, capacity, model_width), 'expert...  68.5 us
    all_to_all x1, waiting for transfers between devices, per_device(): lax.all_to_all(spread_out(sent_x, experts, capacity), 'expert', split_axi...  65.5 us
    all_to_all x1, waiting for transfers between devices, per_device(): lax.all_to_all(parted, 'dp', split_axis=0, concat_axis=0, tiled=True)  40.7 us
    all_gather x1, blocking collectives, per_device(): lax.all_gather(gate_proj, 'dp', axis=1, tiled=True)  32.3 us
    all_gather x1, blocking collectives, per_device(): lax.all_gather(up_proj, 'dp', axis=1, tiled=True)  27.8 us
    all_to_all x1, starting transfers between devices, per_device(): lax.all_to_all(gate_part.reshape(members, capacity), 'expert', split_axis...  18.9 us
    all_to_all x1, starting transfers between devices, per_device(): lax.all_to_all(spread_out(sent_gate, experts, capacity), 'expert', split_...  16.5 us
  transfers between devices with their start and end apart: 6, of which 5 were waited for; matrix products, arithmetic and copies ran while one was open for 6% of the time, Pallas kernels for 0%

commit v1 on v0

v1 whole, which is shorter than its diff:
```python
import jax
import jax.numpy as jnp
from jax import lax
from jax.experimental import pallas as pl
from jax.experimental.pallas import tpu as pltpu
from jax.sharding import PartitionSpec as P

D = 2560
EXPERTS = 8
CAP = 16
SOURCES = 32
OWNERS = 16
OWN_UNITS = 12
PAD_UNITS = OWNERS * 16
PACK = 640
PACKED = 3 * 1920
GATE_LANES = 128
WIDE = D + GATE_LANES
MESH = pl.DeviceIdType.MESH
BF = jnp.bfloat16
F32 = jnp.float32

HOPS = ((1, 0), (3, 0), (0, 1), (2, 0), (1, 1), (3, 1), (2, 1))


def flip(bit):
    return 1 - bit


class Place:
    def __init__(self):
        i, d = lax.axis_index("expert"), lax.axis_index("dp")
        self.yh, self.z = lax.div(i, 8), lax.rem(i, 8)
        self.x, self.yl, self.c = lax.div(d, 4), lax.rem(lax.div(d, 2), 2), lax.rem(d, 2)
        self.zh, self.zl = lax.div(self.z, 4), lax.rem(self.z, 4)
        self.xp, self.xh = lax.rem(self.x, 2), lax.div(self.x, 2)
        self.expert = self.yh * 2 + self.zh
        self.near = self.zl + 1 - 2 * lax.rem(self.zl, 2)
        self.far = lax.rem(self.zl + 2, 4)
        self.x_mate = self.dev(x=self.x + 1 - 2 * self.xp)
        self.c_mate = self.dev(c=flip(self.c))
        self.y_side = self.dev(yl=flip(self.yl))
        self.z_far = self.dev(z=self.zh * 4 + self.far)
        self.z_near = self.dev(z=self.zh * 4 + self.near)
        self.x_side = self.dev(x=3 - self.x)

    def dev(self, x=None, yh=None, yl=None, z=None, c=None):
        x = self.x if x is None else x
        yh = self.yh if yh is None else yh
        yl = self.yl if yl is None else yl
        z = self.z if z is None else z
        c = self.c if c is None else c
        return (yh * 8 + z, (x * 2 + yl) * 2 + c)

    def hop(self, dy, dz):
        yh = lax.rem(self.yh + dy, 4)
        zh = flip(self.zh) if dz else self.zh
        return self.dev(yh=yh, z=7 - self.z if dz else self.z), yh * 2 + zh

    def origin(self, dy, dz):
        yh = lax.rem(self.yh + 4 - dy, 4)
        return yh * 2 + (flip(self.zh) if dz else self.zh)

    def owner(self, xh=None, yl=None, zl=None):
        xh = self.xh if xh is None else xh
        yl = self.yl if yl is None else yl
        zl = self.zl if zl is None else zl
        return (xh * 2 + yl) * 4 + zl

    def greet(self):
        barrier = pltpu.get_barrier_semaphore()
        mates = [self.hop(*h)[0] for h in HOPS] + [
            self.x_mate, self.c_mate, self.y_side, self.z_far, self.z_near, self.x_side,
        ]
        for mate in mates:
            pl.semaphore_signal(barrier, inc=1, device_id=mate, device_id_type=MESH)
        pl.semaphore_wait(barrier, len(mates))


class Sends:
    def __init__(self, sems):
        self.sems, self.open = sems, []

    def start(self, src, dst, recv, device):
        copy = pltpu.make_async_remote_copy(
            src_ref=src, dst_ref=dst, send_sem=self.sems.at[len(self.open)], recv_sem=recv,
            device_id=device, device_id_type=MESH,
        )
        copy.start()
        self.open.append(copy)

    def arrived(self, dst, recv, device):
        pltpu.make_async_remote_copy(
            src_ref=dst, dst_ref=dst, send_sem=self.sems.at[0], recv_sem=recv,
            device_id=device, device_id_type=MESH,
        ).wait_recv()

    def finish(self):
        for copy in self.open:
            copy.wait_send()


def spread_kernel(rows_in, w_in, rows, wall, row_sems, w_sems, send_sems, own_sems):
    me = Place()
    me.greet()
    out = Sends(send_sems)
    own_row = (me.c * 2 + me.xp) * 8 + me.expert
    own_w = me.owner()
    keep = [
        pltpu.make_async_copy(rows_in.at[me.expert], rows.at[own_row], own_sems.at[0]),
        pltpu.make_async_copy(w_in, wall.at[own_w], own_sems.at[1]),
    ]

    def slot(c, xp, origin):
        return (c * 2 + xp) * 8 + origin

    def send_row(src, index, device):
        out.start(src, rows.at[index], row_sems.at[index], device)

    def send_w(src, index, devices):
        for device in devices:
            out.start(src, wall.at[index], w_sems.at[index], device)

    def send_hop(hop):
        device, expert = me.hop(*hop)
        send_row(rows_in.at[expert], own_row, device)

    def take_row(hop):
        index = slot(me.c, me.xp, me.origin(*hop))
        out.arrived(rows.at[index], row_sems.at[index], me.c_mate)
        send_row(rows.at[index], index, me.x_mate)
        send_row(rows.at[index], index, me.c_mate)

    def take_mate(hop):
        index = slot(me.c, flip(me.xp), me.origin(*hop))
        out.arrived(rows.at[index], row_sems.at[index], me.c_mate)
        send_row(rows.at[index], index, me.c_mate)

    def take_w(index, devices):
        out.arrived(wall.at[index], w_sems.at[index], me.c_mate)
        send_w(wall.at[index], index, devices)

    own_hop = (0, 0)
    far_w = [me.z_near, me.x_side]
    near_w = [me.x_side]
    send_w(w_in, own_w, [me.y_side, me.z_far])
    send_hop(HOPS[0])
    send_hop(HOPS[1])
    send_row(rows_in.at[me.expert], own_row, me.x_mate)
    send_w(w_in, own_w, far_w)
    for hop in HOPS[2:]:
        send_hop(hop)
    send_row(rows_in.at[me.expert], own_row, me.c_mate)
    for copy in keep:
        copy.start()

    take_w(me.owner(yl=flip(me.yl)), [me.z_far, me.z_near, me.x_side])
    take_row(HOPS[0])
    take_row(HOPS[1])
    take_w(me.owner(zl=me.far), far_w)
    take_w(me.owner(yl=flip(me.yl), zl=me.far), far_w)
    take_row(HOPS[2])
    take_mate(own_hop)
    take_w(me.owner(zl=me.near), near_w)
    take_w(me.owner(zl=me.near, yl=flip(me.yl)), near_w)
    take_row(HOPS[3])
    take_mate(HOPS[0])
    near_far = me.far + 1 - 2 * lax.rem(me.far, 2)
    take_w(me.owner(zl=near_far), near_w)
    take_w(me.owner(zl=near_far, yl=flip(me.yl)), near_w)
    for k in range(4, 7):
        take_row(HOPS[k])
        take_mate(HOPS[k - 3])
    for k in range(4, 7):
        take_mate(HOPS[k])

    def rest_w(zl, carry):
        for yl in range(2):
            index = me.owner(xh=flip(me.xh), yl=yl, zl=zl)
            out.arrived(wall.at[index], w_sems.at[index], me.c_mate)
        return carry

    lax.fori_loop(0, 4, rest_w, 0)

    def rest_row(k, carry):
        index = flip(me.c) * 16 + k
        out.arrived(rows.at[index], row_sems.at[index], me.c_mate)
        return carry

    lax.fori_loop(0, 16, rest_row, 0)
    for copy in keep:
        copy.wait()
    out.finish()


def collect_kernel(
    part, terms, back, shares,
    from_core, from_mate, to_mate, to_home, wx, wn, wf, wy, sn, sf, sy,
    core_sems, mate_sems, home_sems, w_sems, send_sems,
):
    me = Place()
    me.greet()
    out = Sends(send_sems)
    order = ((0, 0),) + HOPS

    def slot(c, xp, origin):
        return (c * 2 + xp) * 8 + origin

    def add_rows(dst, terms_of):
        def step(k, carry):
            cut = pl.ds(pl.multiple_of(k * 384, 128), 384)
            total = terms_of[0][:, cut].astype(F32)
            for term in terms_of[1:]:
                total = total + term[:, cut].astype(F32)
            dst[:, cut] = total.astype(BF)
            return carry

        lax.fori_loop(0, WIDE // 384, step, 0)

    def add_w(dst, terms_of):
        def step(k, carry):
            cut = pl.ds(pl.multiple_of(k * 640, 128), 640)
            total = terms_of[0][:, cut].astype(F32)
            for term in terms_of[1:]:
                total = total + term[:, cut].astype(F32)
            dst[:, cut] = total.astype(BF)
            return carry

        lax.fori_loop(0, PACKED // 640, step, 0)

    far_near = me.far + 1 - 2 * lax.rem(me.far, 2)
    x_order = [(yl, zl) for zl in (me.near, far_near, me.far, me.zl) for yl in (flip(me.yl), me.yl)]

    def send_x(pairs):
        for yl, zl in pairs:
            out.start(
                terms.at[me.owner(xh=flip(me.xh), yl=yl, zl=zl)], wx.at[yl * 4 + zl],
                w_sems.at[yl * 4 + zl], me.x_side,
            )

    def send_core(xp, hops):
        for hop in hops:
            origin = me.origin(*hop)
            index = xp * 8 + origin
            out.start(
                part.at[slot(flip(me.c), xp, origin)], from_core.at[index], core_sems.at[index],
                me.c_mate,
            )

    send_x(x_order[:4])
    send_core(flip(me.xp), order)
    send_x(x_order[4:])
    send_core(me.xp, order)

    def get(ref, sems, index):
        out.arrived(ref.at[index], sems.at[index], me.c_mate)

    def to_x_mate(k):
        origin = me.origin(*order[k])
        index = flip(me.xp) * 8 + origin
        get(from_core, core_sems, index)
        add_rows(to_mate.at[origin], [part.at[slot(me.c, flip(me.xp), origin)], from_core.at[index]])
        out.start(to_mate.at[origin], from_mate.at[origin], mate_sems.at[origin], me.x_mate)

    def send_home(k):
        origin = me.origin(*order[k])
        index = me.xp * 8 + origin
        get(from_core, core_sems, index)
        get(from_mate, mate_sems, origin)
        sums = [part.at[slot(me.c, me.xp, origin)], from_core.at[index], from_mate.at[origin]]
        if k == 0:
            add_rows(back.at[me.expert], sums)
        else:
            add_rows(to_home.at[origin], sums)
            dy, dz = order[k]
            device, expert = me.hop(4 - dy if dy else 0, dz)
            out.start(to_home.at[origin], back.at[me.expert], home_sems.at[me.expert], device)

    def own(yl, zl):
        return terms.at[me.owner(yl=yl, zl=zl)]

    def near_w(k):
        yl, zl = x_order[k]
        index = yl * 4 + zl
        get(wx, w_sems, index)
        there = yl * 2 + lax.div(zl, 2)
        add_w(sn.at[there], [own(yl, zl), wx.at[index]])
        out.start(sn.at[there], wn.at[there], w_sems.at[8 + there], me.z_near)

    def far_w(k):
        yl, zl = x_order[k]
        index, there = yl * 4 + zl, yl * 2 + lax.div(zl, 2)
        get(wx, w_sems, index)
        out.arrived(wn.at[there], w_sems.at[8 + there], me.c_mate)
        add_w(sf.at[yl], [own(yl, zl), wx.at[index], wn.at[there]])
        out.start(sf.at[yl], wf.at[yl], w_sems.at[12 + yl], me.z_far)

    def last_w(k):
        yl, zl = x_order[k]
        index, there = yl * 4 + zl, yl * 2 + lax.div(zl, 2)
        get(wx, w_sems, index)
        out.arrived(wn.at[there], w_sems.at[8 + there], me.c_mate)
        out.arrived(wf.at[yl], w_sems.at[12 + yl], me.c_mate)
        sums = [own(yl, zl), wx.at[index], wn.at[there], wf.at[yl]]
        if k == 6:
            add_w(sy, sums)
            out.start(sy, wy, w_sems.at[14], me.y_side)
        else:
            out.arrived(wy, w_sems.at[14], me.c_mate)
            add_w(shares, sums + [wy])

    for k in range(4):
        to_x_mate(2 * k)
        to_x_mate(2 * k + 1)
        near_w(k)
    for k in range(1, 5):
        send_home(k)
    far_w(4)
    far_w(5)
    for k in range(5, 8):
        send_home(k)
    last_w(6)
    send_home(0)
    last_w(7)
    for hop in HOPS:
        _, expert = me.hop(*hop)
        get(back, home_sems, expert)
    out.finish()


def picks(k):
    row = lax.broadcasted_iota(jnp.int32, (PAD_UNITS, PAD_UNITS), 0)
    col = lax.broadcasted_iota(jnp.int32, (PAD_UNITS, PAD_UNITS), 1)
    lane = row & 15
    wanted = (row - lane) + 12 + (lane & 3)
    return jnp.where((col == wanted) & ((lane >> 2) == k), 1.0, 0.0).astype(BF)


def units_kernel(rows, wall, part, terms, gate_w, up_w, down_w):
    nt = (((1,), (1,)), ((), ()))
    weights = (gate_w, up_w, down_w)
    put = [picks(k) for k in range(3)]
    for m, w in enumerate(weights):
        last = jnp.zeros((PAD_UNITS, PACK), F32)
        for k in range(3):
            start = m * 1920 + k * PACK
            block = wall[:, :, start : start + PACK].reshape(PAD_UNITS, PACK)
            w[:, k * PACK : (k + 1) * PACK] = block
            last = last + jnp.dot(put[k], block, preferred_element_type=F32)
        w[:, 1920:] = last.astype(BF)

    def stack(lo, start, size):
        return rows[:, lo : lo + 16, start : start + size].reshape(SOURCES * CAP, size)

    pre_gate = jnp.zeros((SOURCES * CAP, PAD_UNITS), F32)
    pre_up = jnp.zeros((SOURCES * CAP, PAD_UNITS), F32)
    grad_hidden = jnp.zeros((SOURCES * CAP, PAD_UNITS), F32)
    for k in range(4):
        x = stack(0, k * PACK, PACK)
        cut = slice(k * PACK, (k + 1) * PACK)
        pre_gate += lax.dot_general(x, gate_w[:, cut], nt, preferred_element_type=F32)
        pre_up += lax.dot_general(x, up_w[:, cut], nt, preferred_element_type=F32)
        grad_hidden += lax.dot_general(
            stack(16, k * PACK, PACK), down_w[:, cut], nt, preferred_element_type=F32
        )
    unit = lax.broadcasted_iota(jnp.int32, (SOURCES * CAP, PAD_UNITS), 1)
    real = (unit & 15) < OWN_UNITS
    sig = jax.nn.sigmoid(pre_gate)
    act = pre_gate * sig
    zero = jnp.zeros_like(pre_gate)
    hidden = jnp.where(real, act * pre_up, zero).astype(BF).astype(F32)
    gpg = jnp.where(real, grad_hidden * pre_up * sig * (1.0 + pre_gate * (1.0 - sig)), zero)
    gpu = jnp.where(real, grad_hidden * act, zero)
    gate_part = jnp.sum(hidden * jnp.where(real, grad_hidden, zero), axis=1, keepdims=True)
    part[:, :, D:] = (
        jnp.broadcast_to(gate_part, (SOURCES * CAP, GATE_LANES))
        .astype(BF)
        .reshape(SOURCES, CAP, GATE_LANES)
    )
    gpg_t, gpu_t, hidden_t = gpg.T.astype(BF), gpu.T.astype(BF), hidden.T.astype(BF)
    gpg, gpu = gpg.astype(BF), gpu.astype(BF)
    for k in range(4):
        cut = slice(k * PACK, (k + 1) * PACK)
        grad = jnp.dot(gpg, gate_w[:, cut], preferred_element_type=F32) + jnp.dot(
            gpu, up_w[:, cut], preferred_element_type=F32
        )
        part[:, :, cut] = grad.astype(BF).reshape(SOURCES, CAP, PACK)
    take = [put[k].astype(F32).T.astype(BF) for k in range(3)]
    for m, (left, lo) in enumerate(((gpg_t, 0), (gpu_t, 0), (hidden_t, 16))):
        last = jnp.dot(left, stack(lo, 1920, PACK), preferred_element_type=F32).astype(BF)
        for k in range(3):
            term = jnp.dot(left, stack(lo, k * PACK, PACK), preferred_element_type=F32)
            term = term + jnp.dot(take[k], last, preferred_element_type=F32)
            start = m * 1920 + k * PACK
            terms[:, :, start : start + PACK] = term.astype(BF).reshape(OWNERS, 16, PACK)


def spread(rows_in, w_in):
    anywhere = pl.BlockSpec(memory_space=pl.ANY)
    dma = pltpu.SemaphoreType.DMA
    return pl.pallas_call(
        spread_kernel,
        out_shape=(
            jax.ShapeDtypeStruct((SOURCES, 2 * CAP, D), BF),
            jax.ShapeDtypeStruct((OWNERS, 16, PACKED), BF),
        ),
        in_specs=[anywhere] * 2,
        out_specs=(anywhere, anywhere),
        scratch_shapes=[dma((SOURCES,)), dma((OWNERS,)), dma((46,)), dma((2,))],
        compiler_params=pltpu.CompilerParams(collective_id=0, has_side_effects=True),
        name="spread",
    )(rows_in, w_in)


def units(rows, wall):
    return pl.pallas_call(
        units_kernel,
        out_shape=(
            jax.ShapeDtypeStruct((SOURCES, CAP, WIDE), BF),
            jax.ShapeDtypeStruct((OWNERS, 16, PACKED), BF),
        ),
        in_specs=[pl.BlockSpec(memory_space=pltpu.VMEM)] * 2,
        out_specs=(pl.BlockSpec(memory_space=pltpu.VMEM),) * 2,
        scratch_shapes=[pltpu.VMEM((PAD_UNITS, D), BF)] * 3,
        compiler_params=pltpu.CompilerParams(vmem_limit_bytes=50 * 2**20),
        name="units",
    )(rows, wall)


def collect(part, terms):
    vmem = pl.BlockSpec(memory_space=pltpu.VMEM)
    dma = pltpu.SemaphoreType.DMA
    row, w = (CAP, WIDE), (16, PACKED)
    return pl.pallas_call(
        collect_kernel,
        out_shape=(
            jax.ShapeDtypeStruct((EXPERTS, CAP, WIDE), BF),
            jax.ShapeDtypeStruct((16, PACKED), BF),
        ),
        in_specs=[vmem] * 2,
        out_specs=(vmem, vmem),
        scratch_shapes=[
            pltpu.VMEM((16, *row), BF), pltpu.VMEM((8, *row), BF), pltpu.VMEM((8, *row), BF),
            pltpu.VMEM((8, *row), BF),
            pltpu.VMEM((8, *w), BF), pltpu.VMEM((4, *w), BF), pltpu.VMEM((2, *w), BF),
            pltpu.VMEM(w, BF),
            pltpu.VMEM((4, *w), BF), pltpu.VMEM((2, *w), BF), pltpu.VMEM(w, BF),
            dma((16,)), dma((8,)), dma((8,)), dma((15,)), dma((46,)),
        ],
        compiler_params=pltpu.CompilerParams(
            collective_id=1, has_side_effects=True, vmem_limit_bytes=40 * 2**20
        ),
        name="collect",
    )(part, terms)


def slot_tables(routes):
    named = routes[:, :, None] == jnp.arange(EXPERTS, dtype=jnp.int32)[None, None, :]
    hits = jnp.sum(named.astype(F32), axis=1).astype(BF)
    rows = routes.shape[0]
    earlier = jnp.tri(rows, rows, -1, dtype=BF)
    before = jnp.dot(earlier, hits, preferred_element_type=F32)
    rank = jnp.sum(jnp.where(named, before[:, None, :], 0.0), axis=2).astype(jnp.int32)
    return jnp.where((routes >= 0) & (rank < CAP), routes * CAP + rank, -1)


def pack(w):
    tail = jnp.concatenate([w[4 * k : 4 * k + 4, 1920:] for k in range(3)], axis=1)
    return jnp.concatenate([w[:, :1920], tail], axis=0)


def unpack(packed):
    tail = jnp.concatenate(
        [packed[12:, k * PACK : (k + 1) * PACK] for k in range(3)], axis=0
    )
    return jnp.concatenate([packed[:12, :1920], tail], axis=1)


def per_device(tokens, cotangent, gates, routes, gate_proj, up_proj, down_proj):
    slot_count = EXPERTS * CAP
    slot_ids = slot_tables(routes)
    picked = slot_ids[None, :, :] == jnp.arange(slot_count, dtype=jnp.int32)[:, None, None]
    place = jnp.any(picked, axis=2).astype(BF)
    gate_of = jnp.sum(jnp.where(picked, gates.astype(F32)[None], 0.0), axis=(1, 2))
    sent_x = jnp.dot(place, tokens, preferred_element_type=F32).astype(BF)
    sent_y = jnp.dot(place, cotangent, preferred_element_type=F32)
    scaled = (gate_of[:, None] * sent_y).astype(BF)
    rows_in = jnp.concatenate(
        [sent_x.reshape(EXPERTS, CAP, D), scaled.reshape(EXPERTS, CAP, D)], axis=1
    )
    w_in = jnp.concatenate([pack(gate_proj[0]), pack(up_proj[0]), pack(down_proj[0])], axis=1)
    rows, wall = spread(rows_in, w_in)
    part, terms = units(rows, wall)
    back, shares = collect(part, terms)
    back = back.reshape(slot_count, WIDE)
    grad_tokens = lax.dot_general(
        place, back[:, :D], (((0,), (0,)), ((), ())), preferred_element_type=F32
    ).astype(BF)
    gate_sum = back[:, D].astype(F32)
    grad_gates = (
        jnp.sum(jnp.where(picked, gate_sum[:, None, None], 0.0), axis=0) / gates.astype(F32)
    )
    grads = [unpack(shares[:, m * 1920 : (m + 1) * 1920])[None] for m in range(3)]
    return grad_tokens, grad_gates, *grads


def solution(mesh):
    rows = P(("expert", "dp"), None)
    units_of = P("expert", "dp", None)
    return jax.shard_map(
        per_device,
        mesh=mesh,
        in_specs=(rows, rows, rows, rows, units_of, units_of, units_of),
        out_specs=(rows, rows, units_of, units_of, units_of),
        check_vma=False,
    )
```

time: 469 us -> 150 us (0.32)
  waiting for transfers between devices: 190 us -> 0 us
  blocking collectives: 156 us -> 0 us
  Pallas kernels: 0 us -> 133 us
  starting transfers between devices: 61 us -> 0 us
  matrix products: 25.3 us -> 2.07 us
  local copies, waits for them, and re-layouts: 19.9 us -> 6.07 us
    all_to_all x6 -> x0, waiting for transfers between devices: 190 us -> none  [the longest x1 68.5 us: per_device(): lax.all_to_all(slot_part.reshape(members, capacity, model_width), 'expert...]
    all_gather x3 -> x0, blocking collectives: 156 us -> none  [the longest x1 95.8 us: per_device(): lax.all_gather(down_proj, 'dp', axis=1, tiled=True)]
    pallas_call x0 -> x3, Pallas kernels: none -> 133 us  [the longest x1 71 us: spread(): pl.pallas_call(spread_kernel, out_shape=(jax.ShapeDtypeStruct((SOURCES, 2...]
    all_to_all x6 -> x0, starting transfers between devices: 61 us -> none  [the longest x1 18.9 us: per_device(): lax.all_to_all(gate_part.reshape(members, capacity), 'expert', split_axis...]
    dot_general x12 -> x4, matrix products: 25.3 us -> 2.07 us  [the longest x1 1.22 us: per_device(): lax.dot_general(place, back[:, :D], (((0,), (0,)), ((), ())), preferred_e...]
    broadcast_in_dim x5 -> x0, local copies, waits for them, and re-layouts: 4.89 us -> none  [the longest x3 4.73 us: spread_out(): jnp.broadcast_to(shaped, (experts, GROUP, capacity) + buffer.shape[1:])]
  transfers between devices with their start and end apart: 6 -> 0, of which waited for: 5 -> 0; matrix products, arithmetic and copies ran while one was open for 6% -> 0% of each run, Pallas kernels for 0% -> 0%
where the time goes in v1:
time: 150 us; the launch traced here: 149 us
  Pallas kernels  133 us (89%)
  other arithmetic  7.6 us (5%)
  local copies, waits for them, and re-layouts  6.07 us (4%)
  matrix products  2.07 us (1%)
    pallas_call x1, Pallas kernels, spread(): pl.pallas_call(spread_kernel, out_shape=(jax.ShapeDtypeStruct((SOURCES, 2...  71 us
    pallas_call x1, Pallas kernels, collect(): pl.pallas_call(collect_kernel, out_shape=(jax.ShapeDtypeStruct((EXPERTS,...  46 us
    pallas_call x1, Pallas kernels, units(): pl.pallas_call(units_kernel, out_shape=(jax.ShapeDtypeStruct((SOURCES, CA...  15.6 us

profile of v1, /device:TPU:1, one launch (start us, length us, event | category | flops | bytes accessed | tf_op | source)
XLA Modules:
  0.0 149.0 jit_solution(137827811511791202)
XLA Ops:
  0.6 0.0 copy-start
  0.6 0.0 copy-start.2
  0.7 0.8 convert_element_type.38
  1.4 0.7 convert_reduce_fusion
  2.1 0.2 fusion.3
  2.3 0.7 select_reduce_fusion.2
  3.0 0.7 and_select_fusion
  3.7 0.1 select_reduce_fusion.1
  3.8 0.8 fusion.10
  4.6 0.8 fusion.8
  5.4 0.8 slice.119
  6.3 0.8 slice.123
  7.1 0.8 slice.127
  8.0 0.7 maximum_maximum_fusion.w_in
  8.7 0.0 copy-done
  8.7 0.3 fusion
  9.0 0.0 copy-done.2
  9.0 0.3 convolution_convert_fusion.1
  9.4 1.2 pad_maximum_fusion.rows_in
  10.6 71.0 %spread.1 = (bf16[32,32,2560]{2,1,0:T(8,128)(2,1)}, bf16[16,16,5760]{2,1,0:T(8,128)(2,1)}) custom-call(bf16[8,32,2560]{2,1,0:T(8,128)(2,1)} %pad_maximum_fusion.rows_in, bf16[16,5760]{1,0:T(8,128)(2,1)} %maximum_maximum_fusion.w_in), custom_call_target="tpu_custom_call" | custom-call | tf_op jit(solution)/shard_map/spread/pallas_call | solution.py:401
  81.6 15.6 %units.1 = (bf16[32,16,2688]{2,1,0:T(8,128)(2,1)S(1)}, bf16[16,16,5760]{2,1,0:T(8,128)(2,1)}) custom-call(bf16[32,32,2560]{2,1,0:T(8,128)(2,1)} %get-tuple-element.11.rows, bf16[16,16,5760]{2,1,0:T(8,128)(2,1)} %get-tuple-element.12.wall), custom_call_target="tpu_custom_call" | custom-call | tf_op jit(solution)/shard_map/units/pallas_call | solution.py:416
  97.2 1.8 %copy-done.1 = bf16[16,16,5760]{2,1,0:T(8,128)(2,1)S(1)} copy-done((bf16[16,16,5760]{2,1,0:T(8,128)(2,1)S(1)}, bf16[16,16,5760]{2,1,0:T(8,128)(2,1)}, u32[]{:S(2)}) %copy-start.1) | copy-done | bytes 2949144
  99.0 46.0 %collect.1 = (bf16[8,16,2688]{2,1,0:T(8,128)(2,1)S(1)}, bf16[16,5760]{1,0:T(8,128)(2,1)S(1)}) custom-call(bf16[32,16,2688]{2,1,0:T(8,128)(2,1)S(1)} %get-tuple-element.13.part, bf16[16,16,5760]{2,1,0:T(8,128)(2,1)S(1)} %copy-done.1), custom_call_target="tpu_custom_call" | custom-call | tf_op jit(solution)/shard_map/collect/pallas_call | solution.py:434
  145.0 0.0 copy-start.3
  145.0 1.2 convolution_convert_fusion
  146.2 0.1 copy.18
  146.3 0.1 select_reduce_fusion
  146.4 0.0 copy-done.3
  146.5 0.6 convert_divide_fusion
  147.1 0.7 maximum_bitcast_fusion.2
  147.7 0.7 maximum_bitcast_fusion.1
  148.4 0.7 maximum_bitcast_fusion
  (7 shorter events, 0.1 us)
Async XLA Ops:
  0.6 8.1 %copy-start = (bf16[128,2560]{1,0:T(8,128)(2,1)S(1)}, bf16[128,2560]{1,0:T(8,128)(2,1)}, u32[]{:S(2)}) copy-start(bf16[128,2560]{1,0:T(8,128)(2,1)} %param.8) | copy-start | bytes 1966084
  0.6 8.4 %copy-start.2 = (bf16[128,2560]{1,0:T(8,128)(2,1)S(1)}, bf16[128,2560]{1,0:T(8,128)(2,1)}, u32[]{:S(2)}) copy-start(bf16[128,2560]{1,0:T(8,128)(2,1)} %param.7) | copy-start | bytes 1966084
  97.2 1.8 %copy-start.1 = (bf16[16,16,5760]{2,1,0:T(8,128)(2,1)S(1)}, bf16[16,16,5760]{2,1,0:T(8,128)(2,1)}, u32[]{:S(2)}) copy-start(bf16[16,16,5760]{2,1,0:T(8,128)(2,1)} %get-tuple-element.14.terms) | copy-start | bytes 8847364
  145.0 1.4 copy-start.3

commit v2 on v1

v2 whole, which is shorter than its diff:
```python
import jax
import jax.numpy as jnp
from jax import lax
from jax.experimental import pallas as pl
from jax.experimental.pallas import tpu as pltpu
from jax.sharding import PartitionSpec as P

D = 2560
EXPERTS = 8
CAP = 16
SOURCES = 32
TOK = 128
HALF = 256
OWNERS = 16
OWN_UNITS = 12
PAD_UNITS = OWNERS * 16
PACK = 640
PACKED = 3 * 1920
GATE_LANES = 128
WIDE = D + GATE_LANES
MESH = pl.DeviceIdType.MESH
BF = jnp.bfloat16
F32 = jnp.float32

HOPS = ((1, 0), (3, 0), (0, 1), (2, 0), (1, 1), (3, 1), (2, 1))


def flip(bit):
    return 1 - bit


class Place:
    def __init__(self):
        i, d = lax.axis_index("expert"), lax.axis_index("dp")
        self.yh, self.z = lax.div(i, 8), lax.rem(i, 8)
        self.x, self.yl, self.c = lax.div(d, 4), lax.rem(lax.div(d, 2), 2), lax.rem(d, 2)
        self.zh, self.zl = lax.div(self.z, 4), lax.rem(self.z, 4)
        self.xp, self.xh = lax.rem(self.x, 2), lax.div(self.x, 2)
        self.expert = self.yh * 2 + self.zh
        self.near = self.zl + 1 - 2 * lax.rem(self.zl, 2)
        self.far = lax.rem(self.zl + 2, 4)
        self.x_mate = self.dev(x=self.x + 1 - 2 * self.xp)
        self.c_mate = self.dev(c=flip(self.c))
        self.y_side = self.dev(yl=flip(self.yl))
        self.z_far = self.dev(z=self.zh * 4 + self.far)
        self.z_near = self.dev(z=self.zh * 4 + self.near)
        self.x_side = self.dev(x=3 - self.x)

    def dev(self, x=None, yh=None, yl=None, z=None, c=None):
        x = self.x if x is None else x
        yh = self.yh if yh is None else yh
        yl = self.yl if yl is None else yl
        z = self.z if z is None else z
        c = self.c if c is None else c
        return (yh * 8 + z, (x * 2 + yl) * 2 + c)

    def hop(self, dy, dz):
        yh = lax.rem(self.yh + dy, 4)
        zh = flip(self.zh) if dz else self.zh
        return self.dev(yh=yh, z=7 - self.z if dz else self.z), yh * 2 + zh

    def origin(self, dy, dz):
        yh = lax.rem(self.yh + 4 - dy, 4)
        return yh * 2 + (flip(self.zh) if dz else self.zh)

    def owner(self, xh=None, yl=None, zl=None):
        xh = self.xh if xh is None else xh
        yl = self.yl if yl is None else yl
        zl = self.zl if zl is None else zl
        return (xh * 2 + yl) * 4 + zl

    def signal(self):
        barrier = pltpu.get_barrier_semaphore()
        mates = [self.hop(*h)[0] for h in HOPS] + [
            self.x_mate, self.c_mate, self.y_side, self.z_far, self.z_near, self.x_side,
        ]
        for mate in mates:
            pl.semaphore_signal(barrier, inc=1, device_id=mate, device_id_type=MESH)
        self.mates = len(mates)

    def meet(self):
        pl.semaphore_wait(pltpu.get_barrier_semaphore(), self.mates)


class Sends:
    def __init__(self, sems):
        self.sems, self.open = sems, []

    def start(self, src, dst, recv, device):
        copy = pltpu.make_async_remote_copy(
            src_ref=src, dst_ref=dst, send_sem=self.sems.at[len(self.open)], recv_sem=recv,
            device_id=device, device_id_type=MESH,
        )
        copy.start()
        self.open.append(copy)

    def arrived(self, dst, recv, device):
        pltpu.make_async_remote_copy(
            src_ref=dst, dst_ref=dst, send_sem=self.sems.at[0], recv_sem=recv,
            device_id=device, device_id_type=MESH,
        ).wait_recv()

    def finish(self):
        for copy in self.open:
            copy.wait_send()


def pick_rows(k):
    row = lax.broadcasted_iota(jnp.int32, (PAD_UNITS, PAD_UNITS), 0)
    col = lax.broadcasted_iota(jnp.int32, (PAD_UNITS, PAD_UNITS), 1)
    lane = row & 15
    wanted = (row - lane) + 12 + (lane & 3)
    return jnp.where((col == wanted) & ((lane >> 2) == k), 1.0, 0.0)


def layer_kernel(
    tokens, cotangent, gates, routes, gate_proj, up_proj, down_proj,
    grad_tokens, grad_gates, grad_gate, grad_up, grad_down,
    rows_in, rows, wall, tails, place_t, picked, acc, left, left_t, part, terms,
    from_core, from_mate, to_mate, to_home, back, wx, wn, wf, wy, sn, sf, sy, shares,
    row_sems, gather_sems, core_sems, mate_sems, home_sems, reduce_sems, send_sems,
):
    me = Place()
    me.signal()
    out = Sends(send_sems)
    own_w = me.owner()
    nt = (((1,), (1,)), ((), ()))

    for m, w in enumerate((gate_proj, up_proj, down_proj)):
        whole = w[0].astype(F32)
        tail = jnp.concatenate([whole[4 * k : 4 * k + 4, 1920:] for k in range(3)], axis=1)
        packed = jnp.concatenate([whole[:, :1920], tail], axis=0)
        wall[own_w, :, m * 1920 : (m + 1) * 1920] = packed.astype(BF)
    me.meet()

    def slot(xp, c, origin):
        return (xp * 2 + c) * 8 + origin

    own_row = slot(me.xp, me.c, me.expert)

    def send_row(src, index, device):
        out.start(src, rows.at[index], row_sems.at[index], device)

    def send_w(index, devices):
        for device in devices:
            out.start(wall.at[index], wall.at[index], gather_sems.at[index], device)

    def send_hop(hop):
        device, expert = me.hop(*hop)
        send_row(rows_in.at[expert], own_row, device)

    def take_row(hop):
        index = slot(me.xp, me.c, me.origin(*hop))
        out.arrived(rows.at[index], row_sems.at[index], me.c_mate)
        send_row(rows.at[index], index, me.x_mate)
        send_row(rows.at[index], index, me.c_mate)

    def take_mate(hop):
        index = slot(flip(me.xp), me.c, me.origin(*hop))
        out.arrived(rows.at[index], row_sems.at[index], me.c_mate)
        send_row(rows.at[index], index, me.c_mate)

    def take_w(index, devices):
        out.arrived(wall.at[index], gather_sems.at[index], me.c_mate)
        send_w(index, devices)

    def take_core(xp):
        def step(k, carry):
            index = slot(xp, flip(me.c), k)
            out.arrived(rows.at[index], row_sems.at[index], me.c_mate)
            return carry

        lax.fori_loop(0, 8, step, 0)

    send_w(own_w, [me.y_side, me.z_far, me.z_near, me.x_side])

    lane = lax.broadcasted_iota(jnp.int32, (TOK, TOK), 1)
    row = lax.broadcasted_iota(jnp.int32, (TOK, TOK), 0)
    named = [routes[:, j : j + 1] == lane for j in range(2)]
    hits = jnp.where(named[0] | named[1], 1.0, 0.0)
    earlier = jnp.where(lane < row, 1.0, 0.0).astype(BF)
    before = jnp.dot(earlier, hits.astype(BF), preferred_element_type=F32)
    gate_t = jnp.zeros((TOK, TOK), F32)
    placed = jnp.zeros((TOK, TOK), F32)
    for j in range(2):
        rank = jnp.sum(jnp.where(named[j], before, 0.0), axis=1, keepdims=True).astype(jnp.int32)
        route = routes[:, j : j + 1]
        ids = jnp.where((route >= 0) & (rank < CAP), route * CAP + rank, -1)
        one = jnp.where(ids == lane, 1.0, 0.0)
        picked[j] = one.astype(BF)
        placed = placed + one
        gate_t = gate_t + one * gates[:, j : j + 1].astype(F32)
    place_t[...] = placed.astype(BF)
    place = placed.T.astype(BF)
    gate_of = jnp.sum(gate_t.T, axis=1, keepdims=True)
    for k in range(4):
        cut = slice(k * PACK, (k + 1) * PACK)
        sent_x = jnp.dot(place, tokens[:, cut], preferred_element_type=F32)
        sent_y = jnp.dot(place, cotangent[:, cut], preferred_element_type=F32)
        rows_in[:, :CAP, cut] = sent_x.astype(BF).reshape(EXPERTS, CAP, PACK)
        rows_in[:, CAP:, cut] = (gate_of * sent_y).astype(BF).reshape(EXPERTS, CAP, PACK)

    for hop in HOPS[:2]:
        send_hop(hop)
    send_row(rows_in.at[me.expert], own_row, me.x_mate)
    for hop in HOPS[2:]:
        send_hop(hop)
    send_row(rows_in.at[me.expert], own_row, me.c_mate)
    rows[own_row] = rows_in[me.expert]

    far_w = [me.z_near, me.x_side]
    near_w = [me.x_side]
    near_far = me.far + 1 - 2 * lax.rem(me.far, 2)
    y_not = flip(me.yl)

    def side_w(k):
        take_w(me.owner(xh=flip(me.xh), yl=k // 4, zl=k % 4), [])

    take_w(me.owner(yl=y_not), [me.z_far, me.z_near, me.x_side])
    take_row(HOPS[0])
    take_row(HOPS[1])
    take_w(me.owner(zl=me.far), far_w)
    take_w(me.owner(yl=y_not, zl=me.far), far_w)
    take_row(HOPS[2])
    take_mate((0, 0))
    take_w(me.owner(zl=me.near), near_w)
    take_w(me.owner(zl=me.near, yl=y_not), near_w)
    take_row(HOPS[3])
    take_mate(HOPS[0])
    take_w(me.owner(zl=near_far), near_w)
    take_w(me.owner(zl=near_far, yl=y_not), near_w)
    for k in range(4, 7):
        take_row(HOPS[k])
        take_mate(HOPS[k - 3])
    for k in range(8):
        side_w(k)
    take_mate(HOPS[4])

    put = [pick_rows(k).astype(BF) for k in range(3)]
    for m in range(3):
        last = jnp.zeros((PAD_UNITS, PACK), F32)
        for k in range(3):
            start = m * 1920 + k * PACK
            block = wall[:, :, start : start + PACK].reshape(PAD_UNITS, PACK)
            last = last + jnp.dot(put[k], block, preferred_element_type=F32)
        tails[m] = last.astype(BF)

    def unit_rows(m, k):
        if k == 3:
            return tails[m]
        start = m * 1920 + k * PACK
        return wall[:, :, start : start + PACK].reshape(PAD_UNITS, PACK)

    def forward(xp, k):
        cut = slice(k * PACK, (k + 1) * PACK)
        sources = pl.ds(xp * 16, 16)
        x = rows[sources, :CAP, cut].reshape(HALF, PACK)
        s = rows[sources, CAP:, cut].reshape(HALF, PACK)
        for m, operand in enumerate((x, x, s)):
            product = lax.dot_general(operand, unit_rows(m, k), nt, preferred_element_type=F32)
            if k == 0:
                acc[m] = product
            else:
                acc[m] += product

    def hidden_units(xp):
        unit = lax.broadcasted_iota(jnp.int32, (HALF, PAD_UNITS), 1)
        real = (unit & 15) < OWN_UNITS
        pre_gate, pre_up, grad_hidden = acc[0], acc[1], acc[2]
        sig = jax.nn.sigmoid(pre_gate)
        activated = pre_gate * sig
        zero = jnp.zeros_like(pre_gate)
        hidden = jnp.where(real, activated * pre_up, zero).astype(BF).astype(F32)
        grad_hidden = jnp.where(real, grad_hidden, zero)
        gpg = jnp.where(
            real, grad_hidden * pre_up * sig * (1.0 + pre_gate * (1.0 - sig)), zero
        )
        gpu = jnp.where(real, grad_hidden * activated, zero)
        gate_part = jnp.sum(hidden * grad_hidden, axis=1, keepdims=True)
        part[pl.ds(xp * 16, 16), :, D:] = (
            jnp.broadcast_to(gate_part, (HALF, GATE_LANES)).astype(BF).reshape(16, CAP, GATE_LANES)
        )
        here = pl.ds(pl.multiple_of(xp * HALF, HALF), HALF)
        for m, value in enumerate((gpg, gpu)):
            left[m, here, :] = value.astype(BF)
        for m, value in enumerate((gpg, gpu, hidden)):
            left_t[m, :, here] = value.T.astype(BF)

    take_core(me.xp)
    forward(me.xp, 0)
    take_mate(HOPS[5])
    forward(me.xp, 1)
    forward(me.xp, 2)
    take_mate(HOPS[6])
    forward(me.xp, 3)
    hidden_units(me.xp)
    take_core(flip(me.xp))
    for k in range(4):
        forward(flip(me.xp), k)
    hidden_units(flip(me.xp))

    take = [pick_rows(k).T.astype(BF) for k in range(3)]
    for m, lo in enumerate((0, 0, CAP)):

        def stack(k):
            return rows[:, lo : lo + CAP, k * PACK : (k + 1) * PACK].reshape(2 * HALF, PACK)

        last = jnp.dot(left_t[m], stack(3), preferred_element_type=F32).astype(BF)
        for k in range(3):
            term = jnp.dot(left_t[m], stack(k), preferred_element_type=F32)
            term = term + jnp.dot(take[k], last, preferred_element_type=F32)
            start = m * 1920 + k * PACK
            terms[:, :, start : start + PACK] = term.astype(BF).reshape(OWNERS, 16, PACK)

    x_order = [(yl, zl) for zl in (me.near, near_far, me.far, me.zl) for yl in (y_not, me.yl)]
    for yl, zl in x_order:
        out.start(
            terms.at[me.owner(xh=flip(me.xh), yl=yl, zl=zl)], wx.at[yl * 4 + zl],
            reduce_sems.at[yl * 4 + zl], me.x_side,
        )

    for k in range(4):
        grad = jnp.dot(left[0], unit_rows(0, k), preferred_element_type=F32)
        grad = grad + jnp.dot(left[1], unit_rows(1, k), preferred_element_type=F32)
        part[:, :, k * PACK : (k + 1) * PACK] = grad.astype(BF).reshape(SOURCES, CAP, PACK)

    order = ((0, 0),) + HOPS
    for xp in (flip(me.xp), me.xp):
        for hop in order:
            origin = me.origin(*hop)
            index = xp * 8 + origin
            out.start(
                part.at[slot(xp, flip(me.c), origin)], from_core.at[index], core_sems.at[index],
                me.c_mate,
            )

    def add(dst, terms_of, size):
        def step(k, carry):
            cut = pl.ds(pl.multiple_of(k * size, 128), size)
            total = terms_of[0][:, cut].astype(F32)
            for term in terms_of[1:]:
                total = total + term[:, cut].astype(F32)
            dst[:, cut] = total.astype(dst.dtype)
            return carry

        lax.fori_loop(0, dst.shape[1] // size, step, 0)

    def get(ref, sems, index):
        out.arrived(ref.at[index], sems.at[index], me.c_mate)

    def to_x_mate(k):
        origin = me.origin(*order[k])
        index = flip(me.xp) * 8 + origin
        get(from_core, core_sems, index)
        mine = part.at[slot(flip(me.xp), me.c, origin)]
        add(to_mate.at[origin], [mine, from_core.at[index]], 384)
        out.start(to_mate.at[origin], from_mate.at[origin], mate_sems.at[origin], me.x_mate)

    def send_home(k):
        origin = me.origin(*order[k])
        index = me.xp * 8 + origin
        get(from_core, core_sems, index)
        get(from_mate, mate_sems, origin)
        sums = [part.at[slot(me.xp, me.c, origin)], from_core.at[index], from_mate.at[origin]]
        if k == 0:
            add(back.at[me.expert], sums, 384)
        else:
            add(to_home.at[origin], sums, 384)
            dy, dz = order[k]
            device, _ = me.hop(4 - dy if dy else 0, dz)
            out.start(to_home.at[origin], back.at[me.expert], home_sems.at[me.expert], device)

    def reduce_w(k):
        yl, zl = x_order[k]
        there = yl * 2 + lax.div(zl, 2)
        sums = [terms.at[me.owner(yl=yl, zl=zl)], wx.at[yl * 4 + zl]]
        get(wx, reduce_sems, yl * 4 + zl)
        if k < 4:
            add(sn.at[there], sums, 640)
            out.start(sn.at[there], wn.at[there], reduce_sems.at[8 + there], me.z_near)
            return
        out.arrived(wn.at[there], reduce_sems.at[8 + there], me.c_mate)
        sums.append(wn.at[there])
        if k < 6:
            add(sf.at[yl], sums, 640)
            out.start(sf.at[yl], wf.at[yl], reduce_sems.at[12 + yl], me.z_far)
            return
        out.arrived(wf.at[yl], reduce_sems.at[12 + yl], me.c_mate)
        sums.append(wf.at[yl])
        if k == 6:
            add(sy, sums, 640)
            out.start(sy, wy, reduce_sems.at[14], me.y_side)
        else:
            out.arrived(wy, reduce_sems.at[14], me.c_mate)
            add(shares, sums + [wy], 640)

    for k in range(4):
        to_x_mate(2 * k)
        to_x_mate(2 * k + 1)
        reduce_w(k)
    for k in range(1, 5):
        send_home(k)
    reduce_w(4)
    reduce_w(5)
    for k in range(5, 8):
        send_home(k)
    send_home(0)
    reduce_w(6)

    for hop in HOPS:
        _, expert = me.hop(*hop)
        get(back, home_sems, expert)
    for k in range(4):
        cut = slice(k * PACK, (k + 1) * PACK)
        block = back[:, :, cut].reshape(TOK, PACK)
        grad_tokens[:, cut] = jnp.dot(
            place_t[...], block, preferred_element_type=F32
        ).astype(BF)
    gate_back = back[:, :, D:].reshape(TOK, GATE_LANES)
    for j in range(2):
        gate_sum = jnp.dot(picked[j], gate_back, preferred_element_type=F32)
        grad_gates[:, j : j + 1] = gate_sum[:, :1] / gates[:, j : j + 1].astype(F32)

    reduce_w(7)
    for m, grad in enumerate((grad_gate, grad_up, grad_down)):
        whole = shares[:, m * 1920 : (m + 1) * 1920]
        grad[0, :, :1920] = whole[:OWN_UNITS].astype(BF)
        tail = jnp.concatenate(
            [whole[OWN_UNITS:, k * PACK : (k + 1) * PACK] for k in range(3)], axis=0
        )
        grad[0, :, 1920:] = tail.astype(BF)
    out.finish()


def per_device(tokens, cotangent, gates, routes, gate_proj, up_proj, down_proj):
    vmem = pl.BlockSpec(memory_space=pltpu.VMEM)
    dma = pltpu.SemaphoreType.DMA
    row, w = (CAP, WIDE), (16, PACKED)
    scratch = [
        ((EXPERTS, 2 * CAP, D), BF), ((SOURCES, 2 * CAP, D), BF), ((OWNERS, *w), BF),
        ((3, PAD_UNITS, PACK), BF), ((TOK, TOK), BF), ((2, TOK, TOK), BF),
        ((3, HALF, PAD_UNITS), F32), ((2, 2 * HALF, PAD_UNITS), BF), ((3, PAD_UNITS, 2 * HALF), BF),
        ((SOURCES, *row), BF), ((OWNERS, *w), BF),
        ((16, *row), BF), ((8, *row), BF), ((8, *row), BF), ((8, *row), BF), ((EXPERTS, *row), BF),
        ((8, *w), BF), ((4, *w), BF), ((2, *w), BF), (w, BF),
        ((4, *w), BF), ((2, *w), BF), (w, BF), (w, F32),
    ]
    shape = jax.ShapeDtypeStruct
    weight = shape(gate_proj.shape, BF)
    return pl.pallas_call(
        layer_kernel,
        out_shape=(
            shape(tokens.shape, BF), shape(gates.shape, F32), weight, weight, weight,
        ),
        in_specs=[vmem] * 7,
        out_specs=(vmem,) * 5,
        scratch_shapes=[pltpu.VMEM(*s) for s in scratch]
        + [dma((n,)) for n in (SOURCES, OWNERS, 16, 8, 8, 15, 92)],
        compiler_params=pltpu.CompilerParams(
            collective_id=0, has_side_effects=True, vmem_limit_bytes=56 * 2**20
        ),
        name="layer",
    )(tokens, cotangent, gates, routes, gate_proj, up_proj, down_proj)


def solution(mesh):
    rows = P(("expert", "dp"), None)
    units_of = P("expert", "dp", None)
    return jax.shard_map(
        per_device,
        mesh=mesh,
        in_specs=(rows, rows, rows, rows, units_of, units_of, units_of),
        out_specs=(rows, rows, units_of, units_of, units_of),
        check_vma=False,
    )
```

time: 150 us -> 135 us (0.900)
  the two profiles are of different devices: /device:TPU:1 before, /device:TPU:32 now
where the time goes in v2:
time: 135 us; the launch traced here: 134 us
  Pallas kernels  126 us (93%)
  local copies, waits for them, and re-layouts  8.08 us (6%)
    pallas_call x1, Pallas kernels, per_device(): pl.pallas_call(layer_kernel, out_shape=(shape(tokens.shape, BF), shape(ga...  126 us
    unnamed x14, local copies, waits for them, and re-layouts  6.6 us

profile of v2, /device:TPU:32, one launch (start us, length us, event | category | flops | bytes accessed | tf_op | source)
XLA Modules:
  0.0 134.4 jit_solution(3142226249265728433)
XLA Ops:
  0.6 0.0 copy-start.3
  0.6 1.4 %copy.12.gates = bf16[128,2]{1,0:T(8,128)(2,1)} copy(bf16[128,2]{0,1:T(2,128)(2,1)} %param.9) | data formatting | bytes 1024 | tf_op args[2]
  2.0 0.0 copy-done.3
  2.0 0.7 copy.13.routes
  2.8 125.7 %layer.1 = (bf16[128,2560]{1,0:T(8,128)(2,1)}, f32[128,2]{1,0:T(8,128)}, bf16[1,12,2560]{2,1,0:T(8,128)(2,1)}, bf16[1,12,2560]{2,1,0:T(8,128)(2,1)}, bf16[1,12,2560]{2,1,0:T(8,128)(2,1)}) custom-call(bf16[128,2560]{1,0:T(8,128)(2,1)} %tokens.1, bf16[128,2560]{1,0:T(8,128)(2,1)} %cotangent.1, bf16[128,2]{1,0:T(8,128)(2,1)} %copy.12.gates, ...), custom_call_target="tpu_custom_call" | custom-call | tf_op jit(solution)/shard_map/layer/pallas_call | solution.py:450
  128.5 1.5 %copy.14 = f32[128,2]{0,1:T(2,128)} copy(f32[128,2]{1,0:T(8,128)} %get-tuple-element.6) | data formatting | bytes 2048 | tf_op jit(solution)/shard_map/layer/pallas_call | solution.py:450
  130.0 0.0 copy-start.2
  130.0 2.0 %copy.19 = bf16[128,2560]{1,0:T(8,128)(2,1)} copy(bf16[128,2560]{1,0:T(8,128)(2,1)} %get-tuple-element.15) | data formatting | bytes 1310720
  132.0 0.0 copy-done.2
  132.0 0.0 copy-start.1
  132.0 0.6 copy.20
  132.6 0.3 copy-done.1
  132.9 0.0 copy-start
  132.9 0.6 copy.21
  133.5 0.3 copy-done
  133.8 0.6 copy.22
Async XLA Ops:
  0.6 1.4 %copy-start.3 = (s32[128,2]{0,1:T(2,128)S(1)}, s32[128,2]{0,1:T(2,128)}, u32[]{:S(2)}) copy-start(s32[128,2]{0,1:T(2,128)} %param.10) | copy-start | bytes 3076
  130.0 2.0 %copy-start.2 = (bf16[1,12,2560]{2,1,0:T(8,128)(2,1)S(1)}, bf16[1,12,2560]{2,1,0:T(8,128)(2,1)}, u32[]{:S(2)}) copy-start(bf16[1,12,2560]{2,1,0:T(8,128)(2,1)} %get-tuple-element.17) | copy-start | bytes 184324
  132.0 0.9 copy-start.1
  132.9 0.9 copy-start

commit v3 on v2

v3 whole, which is shorter than its diff:
```python
import jax
import jax.numpy as jnp
from jax import lax
from jax.experimental import pallas as pl
from jax.experimental.pallas import tpu as pltpu
from jax.sharding import PartitionSpec as P

D = 2560
EXPERTS = 8
CAP = 16
SOURCES = 32
TOK = 128
HALF = 256
OWNERS = 16
OWN_UNITS = 12
PAD_UNITS = OWNERS * 16
PACK = 640
PACKED = 3 * 1920
GATE_LANES = 128
WIDE = D + GATE_LANES
MESH = pl.DeviceIdType.MESH
BF = jnp.bfloat16
F32 = jnp.float32

ROW_WINDOW = 3
SHARD_WINDOW = 8
HOPS = ((1, 0), (3, 0), (0, 1), (2, 0), (1, 1), (3, 1), (2, 1))

ORIGINS = ((1, 0), (2, 0), (0, 1), (3, 0), (1, 1), (2, 1), (3, 1))


def flip(bit):
    return 1 - bit


class Place:
    def __init__(self):
        i, d = lax.axis_index("expert"), lax.axis_index("dp")
        self.yh, self.z = lax.div(i, 8), lax.rem(i, 8)
        self.x, self.yl, self.c = lax.div(d, 4), lax.rem(lax.div(d, 2), 2), lax.rem(d, 2)
        self.zh, self.zl = lax.div(self.z, 4), lax.rem(self.z, 4)
        self.xp, self.xh = lax.rem(self.x, 2), lax.div(self.x, 2)
        self.expert = self.yh * 2 + self.zh
        self.near = self.zl + 1 - 2 * lax.rem(self.zl, 2)
        self.far = lax.rem(self.zl + 2, 4)
        self.mirror = 3 - self.zl
        self.z_near = self.dev(z=self.zh * 4 + self.near)
        self.z_far = self.dev(z=self.zh * 4 + self.far)
        self.x_mate = self.dev(x=self.x + 1 - 2 * self.xp)
        self.c_mate = self.dev(c=flip(self.c))
        self.y_side = self.dev(yl=flip(self.yl))
        self.mirror = 3 - self.zl
        self.x_side = self.dev(x=3 - self.x)

    def dev(self, x=None, yh=None, yl=None, z=None, c=None):
        x = self.x if x is None else x
        yh = self.yh if yh is None else yh
        yl = self.yl if yl is None else yl
        z = self.z if z is None else z
        c = self.c if c is None else c
        return (yh * 8 + z, (x * 2 + yl) * 2 + c)

    def hop(self, dy, dz):
        yh = lax.rem(self.yh + dy, 4)
        zh = flip(self.zh) if dz else self.zh
        yl = (self.yl, 0, flip(self.yl), 1)[dy]
        kind = (0, 1 + self.yl, 3, 1 + self.yl)[dy]
        return self.dev(yh=yh, yl=yl, z=7 - self.z if dz else self.z), yh * 2 + zh, kind

    def origin(self, kind, dz):
        z = 7 - self.z if dz else self.z
        if kind == 0:
            return self.dev(z=z)
        if kind == 3:
            return self.dev(yh=lax.rem(self.yh + 2, 4), yl=flip(self.yl), z=z)
        return self.dev(yh=lax.rem(self.yh + 3 + 2 * self.yl, 4), yl=kind - 1, z=z)

    def owner(self, xh=None, yl=None, zl=None):
        xh = self.xh if xh is None else xh
        yl = self.yl if yl is None else yl
        zl = self.zl if zl is None else zl
        return (xh * 2 + yl) * 4 + zl

    def signal(self):
        barrier = pltpu.get_barrier_semaphore()
        mates = [self.hop(*h)[0] for h in HOPS]
        beside = lax.rem(self.yh + 3 + 2 * self.yl, 4)
        mates += [self.dev(yh=beside, z=z) for z in (self.z, 7 - self.z)]
        mates += [
            self.x_mate, self.c_mate, self.y_side, self.z_near, self.z_far, self.x_side,
        ]
        for mate in mates:
            pl.semaphore_signal(barrier, inc=1, device_id=mate, device_id_type=MESH)
        self.mates = len(mates)

    def meet(self):
        pl.semaphore_wait(pltpu.get_barrier_semaphore(), self.mates)


class Sends:
    def __init__(self, sems):
        self.sems, self.open = sems, []

    def start(self, src, dst, recv, device):
        copy = pltpu.make_async_remote_copy(
            src_ref=src, dst_ref=dst, send_sem=self.sems.at[len(self.open)], recv_sem=recv,
            device_id=device, device_id_type=MESH,
        )
        copy.start()
        self.open.append(copy)

    def arrived(self, dst, recv, device):
        pltpu.make_async_remote_copy(
            src_ref=dst, dst_ref=dst, send_sem=self.sems.at[0], recv_sem=recv,
            device_id=device, device_id_type=MESH,
        ).wait_recv()

    def finish(self):
        for copy in self.open:
            copy.wait_send()


def pick_rows(k):
    row = lax.broadcasted_iota(jnp.int32, (PAD_UNITS, PAD_UNITS), 0)
    col = lax.broadcasted_iota(jnp.int32, (PAD_UNITS, PAD_UNITS), 1)
    lane = row & 15
    wanted = (row - lane) + 12 + (lane & 3)
    return jnp.where((col == wanted) & ((lane >> 2) == k), 1.0, 0.0)


def layer_kernel(
    tokens, cotangent, gates, routes, gate_proj, up_proj, down_proj,
    back, slots, shares,
    rows_in, rows, wall, tails, acc, left, left_t, part, terms,
    from_core, from_mate, to_mate, to_home, wx, wy, wn, wf, sy, sn, sf,
    row_sems, gather_sems, core_sems, mate_sems, home_sems, reduce_sems, send_sems,
):
    me = Place()
    me.signal()
    out = Sends(send_sems)
    own_w = me.owner()
    nt = (((1,), (1,)), ((), ()))

    for m, w in enumerate((gate_proj, up_proj, down_proj)):
        whole = w[0].astype(F32)
        tail = jnp.concatenate([whole[4 * k : 4 * k + 4, 1920:] for k in range(3)], axis=1)
        packed = jnp.concatenate([whole[:, :1920], tail], axis=0)
        wall[own_w, :, m * 1920 : (m + 1) * 1920] = packed.astype(BF)
    me.meet()

    def slot(xp, c, kind, dz):
        return (xp * 2 + c) * 8 + kind * 2 + dz

    own_row = slot(me.xp, me.c, 0, 0)

    def send_row(src, index, device):
        out.start(src, rows.at[index], row_sems.at[index], device)

    def send_w(index, devices):
        for device in devices:
            out.start(wall.at[index], wall.at[index], gather_sems.at[index], device)

    def send_hop(hop):
        device, expert, kind = me.hop(*hop)
        send_row(rows_in.at[expert], slot(me.xp, me.c, kind, hop[1]), device)

    def take_row(source):
        index = slot(me.xp, me.c, *source)
        out.arrived(rows.at[index], row_sems.at[index], me.c_mate)
        send_row(rows.at[index], index, me.x_mate)
        send_row(rows.at[index], index, me.c_mate)

    def take_mate(source):
        index = slot(flip(me.xp), me.c, *source)
        out.arrived(rows.at[index], row_sems.at[index], me.c_mate)
        send_row(rows.at[index], index, me.c_mate)

    def take_w(index, devices):
        out.arrived(wall.at[index], gather_sems.at[index], me.c_mate)
        send_w(index, devices)

    def take_core(xp):
        def step(k, carry):
            index = slot(xp, flip(me.c), 0, 0) + k
            out.arrived(rows.at[index], row_sems.at[index], me.c_mate)
            return carry

        lax.fori_loop(0, 8, step, 0)

    send_w(own_w, [me.z_far, me.z_near, me.y_side, me.x_side])

    lane = lax.broadcasted_iota(jnp.int32, (TOK, TOK), 1)
    row = lax.broadcasted_iota(jnp.int32, (TOK, TOK), 0)
    named = [routes[j : j + 1, :] == row for j in range(2)]
    hits = jnp.where(named[0] | named[1], 1.0, 0.0)
    earlier = jnp.where(row < lane, 1.0, 0.0).astype(BF)
    before = jnp.dot(hits.astype(BF), earlier, preferred_element_type=F32)
    gate_of = jnp.zeros((TOK, TOK), F32)
    place = jnp.zeros((TOK, TOK), F32)
    for j in range(2):
        rank = jnp.sum(jnp.where(named[j], before, 0.0), axis=0, keepdims=True).astype(jnp.int32)
        route = routes[j : j + 1, :]
        ids = jnp.where((route >= 0) & (rank < CAP), route * CAP + rank, -1)
        slots[j : j + 1, :] = ids
        one = jnp.where(ids == row, 1.0, 0.0)
        place = place + one
        gate_of = gate_of + one * gates[j : j + 1, :].astype(F32)
    place = place.astype(BF)
    gate_of = jnp.sum(gate_of, axis=1, keepdims=True)
    for k in range(4):
        cut = slice(k * PACK, (k + 1) * PACK)
        sent_x = jnp.dot(place, tokens[:, cut], preferred_element_type=F32)
        sent_y = jnp.dot(place, cotangent[:, cut], preferred_element_type=F32)
        rows_in[:, :CAP, cut] = sent_x.astype(BF).reshape(EXPERTS, CAP, PACK)
        rows_in[:, CAP:, cut] = (gate_of * sent_y).astype(BF).reshape(EXPERTS, CAP, PACK)

    y_not, x_not = flip(me.yl), flip(me.xh)
    pending = list(HOPS)

    def next_hop():
        if pending:
            send_hop(pending.pop(0))

    next_hop()
    send_row(rows_in.at[me.expert], own_row, me.x_mate)
    for _ in range(ROW_WINDOW - 1):
        next_hop()
    send_row(rows_in.at[me.expert], own_row, me.c_mate)
    rows[own_row] = rows_in[me.expert]

    def row(k):
        take_row(ORIGINS[k])
        next_hop()

    def mate(k):
        take_mate(ORIGINS[k - 1] if k else (0, 0))

    def line(k):
        zl = (me.far, me.near, me.mirror)[k]
        take_w(me.owner(zl=zl), [me.z_near] * (k == 0) + [me.y_side, me.x_side])

    def across(k):
        take_w(me.owner(yl=y_not, zl=(me.zl, me.far, me.near, me.mirror)[k]), [me.x_side])

    def side(k):
        take_w(me.owner(xh=x_not, yl=k // 4, zl=k % 4), [])

    line(1)
    line(0)
    across(0)
    row(0)
    mate(0)
    line(2)
    row(1)
    mate(1)
    across(2)
    row(2)
    across(1)
    mate(2)
    row(3)
    across(3)
    mate(3)
    row(4)
    mate(4)
    row(5)
    row(6)
    for k in range(8):
        side(k)
    mate(5)

    put = [pick_rows(k).astype(BF) for k in range(3)]
    for m in range(3):
        last = jnp.zeros((PAD_UNITS, PACK), F32)
        for k in range(3):
            start = m * 1920 + k * PACK
            block = wall[:, :, start : start + PACK].reshape(PAD_UNITS, PACK)
            last = last + jnp.dot(put[k], block, preferred_element_type=F32)
        tails[m] = last.astype(BF)

    def unit_rows(m, k):
        if k == 3:
            return tails[m]
        start = m * 1920 + k * PACK
        return wall[:, :, start : start + PACK].reshape(PAD_UNITS, PACK)

    def forward(xp, k):
        cut = slice(k * PACK, (k + 1) * PACK)
        sources = pl.ds(xp * 16, 16)
        x = rows[sources, :CAP, cut].reshape(HALF, PACK)
        s = rows[sources, CAP:, cut].reshape(HALF, PACK)
        for m, operand in enumerate((x, x, s)):
            product = lax.dot_general(operand, unit_rows(m, k), nt, preferred_element_type=F32)
            if k == 0:
                acc[m] = product
            else:
                acc[m] += product

    def hidden_units(xp):
        unit = lax.broadcasted_iota(jnp.int32, (HALF, PAD_UNITS), 1)
        real = (unit & 15) < OWN_UNITS
        pre_gate, pre_up, grad_hidden = acc[0], acc[1], acc[2]
        sig = jax.nn.sigmoid(pre_gate)
        activated = pre_gate * sig
        zero = jnp.zeros_like(pre_gate)
        hidden = jnp.where(real, activated * pre_up, zero).astype(BF).astype(F32)
        grad_hidden = jnp.where(real, grad_hidden, zero)
        gpg = jnp.where(
            real, grad_hidden * pre_up * sig * (1.0 + pre_gate * (1.0 - sig)), zero
        )
        gpu = jnp.where(real, grad_hidden * activated, zero)
        gate_part = jnp.sum(hidden * grad_hidden, axis=1, keepdims=True)
        part[pl.ds(xp * 16, 16), :, D:] = (
            jnp.broadcast_to(gate_part, (HALF, GATE_LANES)).astype(BF).reshape(16, CAP, GATE_LANES)
        )
        here = pl.ds(pl.multiple_of(xp * HALF, HALF), HALF)
        for m, value in enumerate((gpg, gpu)):
            left[m, here, :] = value.astype(BF)
        for m, value in enumerate((gpg, gpu, hidden)):
            left_t[m, :, here] = value.T.astype(BF)

    take_core(me.xp)
    forward(me.xp, 0)
    mate(6)
    forward(me.xp, 1)
    forward(me.xp, 2)
    mate(7)
    forward(me.xp, 3)
    hidden_units(me.xp)
    take_core(flip(me.xp))
    for k in range(4):
        forward(flip(me.xp), k)
    hidden_units(flip(me.xp))

    take = [pick_rows(k).T.astype(BF) for k in range(3)]
    for m, lo in enumerate((0, 0, CAP)):

        def stack(k):
            return rows[:, lo : lo + CAP, k * PACK : (k + 1) * PACK].reshape(2 * HALF, PACK)

        last = jnp.dot(left_t[m], stack(3), preferred_element_type=F32).astype(BF)
        for k in range(3):
            term = jnp.dot(left_t[m], stack(k), preferred_element_type=F32)
            term = term + jnp.dot(take[k], last, preferred_element_type=F32)
            start = m * 1920 + k * PACK
            terms[:, :, start : start + PACK] = term.astype(BF).reshape(OWNERS, 16, PACK)

    x_order = [(yl, zl) for yl in (y_not, me.yl) for zl in (me.near, me.mirror, me.far, me.zl)]
    unsent = list(x_order)

    def next_shard():
        if unsent:
            yl, zl = unsent.pop(0)
            index = yl * 4 + zl
            out.start(
                terms.at[me.owner(xh=x_not, yl=yl, zl=zl)], wx.at[index], reduce_sems.at[index],
                me.x_side,
            )

    for _ in range(SHARD_WINDOW):
        next_shard()

    for k in range(4):
        grad = jnp.dot(left[0], unit_rows(0, k), preferred_element_type=F32)
        grad = grad + jnp.dot(left[1], unit_rows(1, k), preferred_element_type=F32)
        part[:, :, k * PACK : (k + 1) * PACK] = grad.astype(BF).reshape(SOURCES, CAP, PACK)

    order = ((0, 0),) + ORIGINS
    for xp in (flip(me.xp), me.xp):
        for kind, dz in order:
            index = xp * 8 + kind * 2 + dz
            out.start(
                part.at[slot(xp, flip(me.c), kind, dz)], from_core.at[index], core_sems.at[index],
                me.c_mate,
            )

    def add(dst, terms_of, size):
        def step(k, carry):
            cut = pl.ds(pl.multiple_of(k * size, 128), size)
            total = terms_of[0][:, cut].astype(F32)
            for term in terms_of[1:]:
                total = total + term[:, cut].astype(F32)
            dst[:, cut] = total.astype(dst.dtype)
            return carry

        lax.fori_loop(0, dst.shape[1] // size, step, 0)

    def get(ref, sems, index):
        out.arrived(ref.at[index], sems.at[index], me.c_mate)

    def to_x_mate(k):
        kind, dz = order[k]
        place = kind * 2 + dz
        index = flip(me.xp) * 8 + place
        get(from_core, core_sems, index)
        mine = part.at[slot(flip(me.xp), me.c, kind, dz)]
        add(to_mate.at[place], [mine, from_core.at[index]], 384)
        out.start(to_mate.at[place], from_mate.at[place], mate_sems.at[place], me.x_mate)

    def send_home(k):
        kind, dz = order[k]
        place = kind * 2 + dz
        index = me.xp * 8 + place
        get(from_core, core_sems, index)
        get(from_mate, mate_sems, place)
        sums = [part.at[slot(me.xp, me.c, kind, dz)], from_core.at[index], from_mate.at[place]]
        if k == 0:
            add(back.at[me.expert], sums, 384)
        else:
            add(to_home.at[place], sums, 384)
            out.start(
                to_home.at[place], back.at[me.expert], home_sems.at[me.expert],
                me.origin(kind, dz),
            )

    def reduce_w(k):
        yl, zl = x_order[k]
        index = yl * 4 + zl
        sums = [terms.at[me.owner(yl=yl, zl=zl)], wx.at[index]]
        get(wx, reduce_sems, index)
        next_shard()
        if k < 4:
            add(sy.at[k], sums, 640)
            out.start(sy.at[k], wy.at[zl], reduce_sems.at[8 + zl], me.y_side)
            return
        out.arrived(wy.at[zl], reduce_sems.at[8 + zl], me.c_mate)
        sums.append(wy.at[zl])
        half = lax.div(zl, 2)
        if k < 6:
            add(sn.at[k - 4], sums, 640)
            out.start(sn.at[k - 4], wn.at[half], reduce_sems.at[12 + half], me.z_near)
            return
        out.arrived(wn.at[half], reduce_sems.at[12 + half], me.c_mate)
        sums.append(wn.at[half])
        if k == 6:
            add(sf, sums, 640)
            out.start(sf, wf, reduce_sems.at[14], me.z_far)
        else:
            out.arrived(wf, reduce_sems.at[14], me.c_mate)
            add(shares, sums + [wf], 640)

    for k in range(4):
        to_x_mate(2 * k)
        to_x_mate(2 * k + 1)
        reduce_w(k)
    for k in range(1, 5):
        send_home(k)
    reduce_w(4)
    for k in range(5, 8):
        send_home(k)
    reduce_w(5)
    send_home(0)
    reduce_w(6)
    for hop in HOPS:
        _, expert, _ = me.hop(*hop)
        get(back, home_sems, expert)
    reduce_w(7)
    out.finish()


def settle_kernel(back, slots, shares, gates, grad_tokens, grad_gates, grad_gate, grad_up, grad_down):
    row = lax.broadcasted_iota(jnp.int32, (TOK, TOK), 0)
    place = jnp.zeros((TOK, TOK), F32)
    gate_back = back[:, :, D:].reshape(TOK, GATE_LANES).astype(F32)
    for j in range(2):
        one = jnp.where(slots[j : j + 1, :] == row, 1.0, 0.0)
        place = place + one
        gate_sum = jnp.sum(one * gate_back, axis=0, keepdims=True)
        grad_gates[j : j + 1, :] = gate_sum / gates[j : j + 1, :].astype(F32)
    place_t = place.T.astype(BF)
    for k in range(4):
        cut = slice(k * PACK, (k + 1) * PACK)
        block = back[:, :, cut].reshape(TOK, PACK)
        grad_tokens[:, cut] = jnp.dot(place_t, block, preferred_element_type=F32).astype(BF)
    for m, grad in enumerate((grad_gate, grad_up, grad_down)):
        whole = shares[:, m * 1920 : (m + 1) * 1920]
        grad[0, :, :1920] = whole[:OWN_UNITS].astype(BF)
        tail = jnp.concatenate(
            [whole[OWN_UNITS:, k * PACK : (k + 1) * PACK] for k in range(3)], axis=0
        )
        grad[0, :, 1920:] = tail.astype(BF)


def per_device(tokens, cotangent, gates, routes, gate_proj, up_proj, down_proj):
    vmem = pl.BlockSpec(memory_space=pltpu.VMEM)
    dma = pltpu.SemaphoreType.DMA
    row, w = (CAP, WIDE), (16, PACKED)
    scratch = [
        ((EXPERTS, 2 * CAP, D), BF), ((SOURCES, 2 * CAP, D), BF), ((OWNERS, *w), BF),
        ((3, PAD_UNITS, PACK), BF),
        ((3, HALF, PAD_UNITS), F32), ((2, 2 * HALF, PAD_UNITS), BF), ((3, PAD_UNITS, 2 * HALF), BF),
        ((SOURCES, *row), BF), ((OWNERS, *w), BF),
        ((16, *row), BF), ((8, *row), BF), ((8, *row), BF), ((8, *row), BF),
        ((8, *w), BF), ((4, *w), BF), ((2, *w), BF), (w, BF), ((4, *w), BF), ((2, *w), BF), (w, BF),
    ]
    shape = jax.ShapeDtypeStruct
    weight = shape(gate_proj.shape, BF)
    gates_t, routes_t = gates.T, routes.T
    back, slots, shares = pl.pallas_call(
        layer_kernel,
        out_shape=(
            shape((EXPERTS, *row), BF), shape((2, TOK), jnp.int32), shape(w, F32),
        ),
        in_specs=[vmem] * 7,
        out_specs=(vmem,) * 3,
        scratch_shapes=[pltpu.VMEM(*s) for s in scratch]
        + [dma((n,)) for n in (SOURCES, OWNERS, 16, 8, 8, 15, 92)],
        compiler_params=pltpu.CompilerParams(
            collective_id=0, has_side_effects=True, vmem_limit_bytes=56 * 2**20
        ),
        name="layer",
    )(tokens, cotangent, gates_t, routes_t, gate_proj, up_proj, down_proj)
    grad_tokens, grad_gates, *grads = pl.pallas_call(
        settle_kernel,
        out_shape=(
            shape(tokens.shape, BF), shape((2, TOK), F32), weight, weight, weight,
        ),
        in_specs=[vmem] * 4,
        out_specs=(vmem,) * 5,
        name="settle",
    )(back, slots, shares, gates_t)
    return grad_tokens, grad_gates.T, *grads


def solution(mesh):
    rows = P(("expert", "dp"), None)
    units_of = P("expert", "dp", None)
    return jax.shard_map(
        per_device,
        mesh=mesh,
        in_specs=(rows, rows, rows, rows, units_of, units_of, units_of),
        out_specs=(rows, rows, units_of, units_of, units_of),
        check_vma=False,
    )
```

time: 135 us -> 127 us (0.941)
  the two profiles are of different devices: /device:TPU:32 before, /device:TPU:1 now
where the time goes in v3:
time: 127 us
  Pallas kernels  126 us (99%)
    pallas_call x1, Pallas kernels, per_device(): pl.pallas_call(layer_kernel, out_shape=(shape((EXPERTS, *row), BF), shape...  124 us

profile of v3, /device:TPU:1, one launch (start us, length us, event | category | flops | bytes accessed | tf_op | source)
XLA Modules:
  0.0 127.0 jit_solution(16637563799335354343)
XLA Ops:
  0.6 123.9 %layer.1 = (bf16[8,16,2688]{2,1,0:T(8,128)(2,1)}, s32[2,128]{1,0:T(2,128)}, f32[16,5760]{1,0:T(8,128)}) custom-call(bf16[128,2560]{1,0:T(8,128)(2,1)} %tokens.1, bf16[128,2560]{1,0:T(8,128)(2,1)} %cotangent.1, bf16[2,128]{1,0:T(2,128)(2,1)} %bitcast.3, s32[2,128]{1,0:T(2,128)} %bitcast.5, bf16[1,12,2560]{2,1,0:T(8,128)(2,1)} %gate_proj.1, ...), custom_call_target="tpu_custom_call" | custom-call | tf_op jit(solution)/shard_map/layer/pallas_call | solution.py:498
  124.6 2.4 %settle.1 = (bf16[128,2560]{1,0:T(8,128)(2,1)}, f32[2,128]{1,0:T(2,128)}, bf16[1,12,2560]{2,1,0:T(8,128)(2,1)}, bf16[1,12,2560]{2,1,0:T(8,128)(2,1)}, bf16[1,12,2560]{2,1,0:T(8,128)(2,1)}) custom-call(bf16[8,16,2688]{2,1,0:T(8,128)(2,1)} %get-tuple-element.13.back, s32[2,128]{1,0:T(2,128)} %get-tuple-element.14.slots, f32[16,5760]{1,0:T(8,128)} %get-tuple-element.15.shares, ...), custom_call_target="tpu_custom_call" | custom-call | tf_op jit(solution)/shard_map/settle/pallas_call | solution.py:512

commit v4 on v3

--- a/solution.py
+++ b/solution.py
@@ -441,12 +441,18 @@
     for k in range(4):
         to_x_mate(2 * k)
         to_x_mate(2 * k + 1)
-        reduce_w(k)
-    for k in range(1, 5):
-        send_home(k)
+    reduce_w(0)
+    send_home(1)
+    send_home(2)
+    reduce_w(1)
+    send_home(3)
+    send_home(4)
+    reduce_w(2)
+    send_home(5)
+    send_home(6)
+    reduce_w(3)
+    send_home(7)
     reduce_w(4)
-    for k in range(5, 8):
-        send_home(k)
     reduce_w(5)
     send_home(0)
     reduce_w(6)

time: 127 us -> 125 us (0.984); the launches traced: 127 us -> 123 us
  Pallas kernels: 126 us -> 123 us
    pallas_call x1, Pallas kernels: 124 us -> 120 us  [per_device(): pl.pallas_call(layer_kernel, out_shape=(shape((EXPERTS, *row), BF), shape...]
where the time goes in v4:
time: 125 us; the launch traced here: 123 us
  Pallas kernels  123 us (98%)
    pallas_call x1, Pallas kernels, per_device(): pl.pallas_call(layer_kernel, out_shape=(shape((EXPERTS, *row), BF), shape...  120 us

profile of v4, /device:TPU:1, one launch (start us, length us, event | category | flops | bytes accessed | tf_op | source)
XLA Modules:
  0.0 123.3 jit_solution(8351905903539956288)
XLA Ops:
  0.6 120.2 %layer.1 = (bf16[8,16,2688]{2,1,0:T(8,128)(2,1)}, s32[2,128]{1,0:T(2,128)}, f32[16,5760]{1,0:T(8,128)}) custom-call(bf16[128,2560]{1,0:T(8,128)(2,1)} %tokens.1, bf16[128,2560]{1,0:T(8,128)(2,1)} %cotangent.1, bf16[2,128]{1,0:T(2,128)(2,1)} %bitcast.3, s32[2,128]{1,0:T(2,128)} %bitcast.5, bf16[1,12,2560]{2,1,0:T(8,128)(2,1)} %gate_proj.1, ...), custom_call_target="tpu_custom_call" | custom-call | tf_op jit(solution)/shard_map/layer/pallas_call | solution.py:504
  120.8 2.4 %settle.1 = (bf16[128,2560]{1,0:T(8,128)(2,1)}, f32[2,128]{1,0:T(2,128)}, bf16[1,12,2560]{2,1,0:T(8,128)(2,1)}, bf16[1,12,2560]{2,1,0:T(8,128)(2,1)}, bf16[1,12,2560]{2,1,0:T(8,128)(2,1)}) custom-call(bf16[8,16,2688]{2,1,0:T(8,128)(2,1)} %get-tuple-element.13.back, s32[2,128]{1,0:T(2,128)} %get-tuple-element.14.slots, f32[16,5760]{1,0:T(8,128)} %get-tuple-element.15.shares, ...), custom_call_target="tpu_custom_call" | custom-call | tf_op jit(solution)/shard_map/settle/pallas_call | solution.py:518
